TPU v7x, 32 devices: a whole 2x2x4 slice. The times are simulated.
32 devices in a mesh: dp: 16 (over z, y, core), seq: 2 (over x).
Axes of the slice: x: 2, y: 2, z: 4, core: 2. Of those that a mesh axis runs over, the one named last changes fastest.
Arguments:
- inputs: bfloat16 [32, 336, 1152], P('dp', 'seq'), may hold values from -6 to 6
- skipped: bfloat16 [32, 336, 1152], P('dp', None, 'seq'), may hold values from -6 to 6
- lengths: int32 [32], P('dp'), may hold values from 1 to 77, as said below
- cotangent: bfloat16 [32, 336, 1152], P('dp', 'seq'), may hold values from -6 to 6
- skip_weight: bfloat16 [2304, 1152], replicated, may hold values from -0.125 to 0.125
- skip_bias: float32 [1152], replicated, may hold values from -3 to 3
- gain_one: float32 [1152], replicated, may hold values from 0.25 to 1.75
- shift_one: float32 [1152], replicated, may hold values from -1.75 to 1.75
- qkv_weight: bfloat16 [1152, 3456], replicated, may hold values from -0.1875 to 0.1875
- proj_weight: bfloat16 [1152, 1152], replicated, may hold values from -0.75 to 0.75
- proj_bias: float32 [1152], replicated, may hold values from -1.75 to 1.75
- gain_two: float32 [1152], replicated, may hold values from 0.25 to 1.75
- shift_two: float32 [1152], replicated, may hold values from -1.75 to 1.75
- fc1_weight: bfloat16 [1152, 4608], replicated, may hold values from -0.1875 to 0.1875
- fc1_bias: float32 [4608], replicated, may hold values from -3 to 3
- fc2_weight: bfloat16 [4608, 1152], replicated, may hold values from -0.09375 to 0.09375
- fc2_bias: float32 [1152], replicated, may hold values from -3 to 3
Outputs:
- block_output: bfloat16 [32, 336, 1152], P('dp', 'seq')
- grad_inputs: float32 [32, 336, 1152], P('dp', 'seq')
- grad_skipped: float32 [32, 336, 1152], P('dp', None, 'seq')
- grad_skip_weight: float32 [2304, 1152], P(('dp', 'seq'))
- grad_skip_bias: float32 [1152], P(('dp', 'seq'))
- grad_gain_one: float32 [1152], P(('dp', 'seq'))
- grad_shift_one: float32 [1152], P(('dp', 'seq'))
- grad_qkv_weight: float32 [1152, 3456], P(('dp', 'seq'))
- grad_proj_weight: float32 [1152, 1152], P(('dp', 'seq'))
- grad_proj_bias: float32 [1152], P(('dp', 'seq'))
- grad_gain_two: float32 [1152], P(('dp', 'seq'))
- grad_shift_two: float32 [1152], P(('dp', 'seq'))
- grad_fc1_weight: float32 [1152, 4608], P(('dp', 'seq'))
- grad_fc1_bias: float32 [4608], P(('dp', 'seq'))
- grad_fc2_weight: float32 [4608, 1152], P(('dp', 'seq'))
- grad_fc2_bias: float32 [1152], P(('dp', 'seq'))
Inputs may be any that keep to these rules, and one draw needn't show every extreme that they name: `lengths`: caption tokens of each item; some item has exactly 77.
All inputs are finite; a program needn't handle non-finite values.
Results may differ from a plain program's by a relative error of at most 0.014.
Values may be sent and summed in bfloat16 or wider, within the bound.
A program may use at most 320 MiB of HBM per device.

v0:
```python
import jax
import jax.numpy as jnp
from jax import lax
from jax.sharding import PartitionSpec as P

HEADS = 16
HEAD_DIM = 72
CAPTION = 77
IMAGE = 256


epsilon = 1e-05
masked_score = -1e30


def layer_norm(stream, gain, shift):
    center = stream - jnp.mean(stream, axis=-1, keepdims=True)
    spread = jnp.mean(center * center, axis=-1, keepdims=True)
    return center * lax.rsqrt(spread + epsilon) * gain + shift


def gelu_exact(values):
    return jax.nn.gelu(values, approximate=False)


def column_sum(values):
    return jnp.sum(values.astype(jnp.float32), axis=0)


def local(
    inputs,
    skipped,
    lengths,
    cotangent,
    skip_weight,
    skip_bias,
    gain_one,
    shift_one,
    qkv_weight,
    proj_weight,
    proj_bias,
    gain_two,
    shift_two,
    fc1_weight,
    fc1_bias,
    fc2_weight,
    fc2_bias,
):
    items, half, width = inputs.shape
    seq_count = lax.axis_size("seq")
    seq_index = lax.axis_index("seq")
    slots = half * seq_count
    first_slot = seq_index * half
    whole_skip = lax.all_gather(skipped, "seq", axis=2, tiled=True)
    own_skip = lax.dynamic_slice_in_dim(whole_skip, first_slot, half, 1)
    rows = items * half
    joined = jnp.concatenate([inputs, own_skip], axis=-1).reshape(rows, 2 * width)
    stream = jnp.dot(joined, skip_weight, preferred_element_type=jnp.float32) + skip_bias
    normed = layer_norm(stream, gain_one, shift_one).astype(jnp.bfloat16)
    packed = jnp.dot(normed, qkv_weight, preferred_element_type=jnp.float32).astype(jnp.bfloat16)
    packed = packed.reshape(items, half, 3 * width)
    query = packed[:, :, :width]
    own_keys = packed[:, :, width : 2 * width]
    own_values = packed[:, :, 2 * width :]
    all_keys, all_values = (
        lax.all_gather(own_keys, "seq", axis=1, tiled=True),
        lax.all_gather(own_values, "seq", axis=1, tiled=True),
    )
    query_heads = query.reshape(items, half, HEADS, HEAD_DIM)
    key_heads = all_keys.reshape(items, slots, HEADS, HEAD_DIM)
    value_heads = all_values.reshape(items, slots, HEADS, HEAD_DIM)
    scale = HEAD_DIM ** (-0.5)
    positions = jnp.arange(slots, dtype=jnp.int32)[None, :]
    caption = (positions >= 1) & (positions <= lengths[:, None])
    image = (positions >= 1 + CAPTION) & (positions < 1 + CAPTION + IMAGE)
    valid = (positions == 0) | caption | image
    scores = (
        jnp.einsum("iqhd,ikhd->ihqk", query_heads, key_heads, preferred_element_type=jnp.float32)
        * scale
    )
    scores = jnp.where(valid[:, None, None, :], scores, masked_score)
    top = jnp.max(scores, axis=-1, keepdims=True)
    expo = jnp.exp(scores - top)
    probs = expo / jnp.sum(expo, axis=-1, keepdims=True)
    probs_low = probs.astype(jnp.bfloat16)
    mixed = jnp.einsum(
        "ihqk,ikhd->iqhd", probs_low, value_heads, preferred_element_type=jnp.float32
    )
    mixed = mixed.astype(jnp.bfloat16).reshape(rows, width)
    attended = jnp.dot(mixed, proj_weight, preferred_element_type=jnp.float32) + proj_bias
    stream_two = stream + attended
    normed_two = layer_norm(stream_two, gain_two, shift_two).astype(jnp.bfloat16)
    hidden = jnp.dot(normed_two, fc1_weight, preferred_element_type=jnp.float32) + fc1_bias
    acted, gelu_back = jax.vjp(gelu_exact, hidden)
    acted_low = acted.astype(jnp.bfloat16)
    result = stream_two + (
        jnp.dot(acted_low, fc2_weight, preferred_element_type=jnp.float32) + fc2_bias
    )
    block_output = result.astype(jnp.bfloat16).reshape(items, half, width)
    grad_out = cotangent.reshape(rows, width)
    grad_fc2_weight = jnp.dot(acted_low.T, grad_out, preferred_element_type=jnp.float32)
    grad_fc2_bias = column_sum(grad_out)
    grad_acted = jnp.dot(grad_out, fc2_weight.T, preferred_element_type=jnp.float32)
    grad_hidden = gelu_back(grad_acted)[0].astype(jnp.bfloat16)
    grad_fc1_weight = jnp.dot(normed_two.T, grad_hidden, preferred_element_type=jnp.float32)
    grad_fc1_bias = column_sum(grad_hidden)
    grad_normed_two = jnp.dot(grad_hidden, fc1_weight.T, preferred_element_type=jnp.float32)
    norm_out_two, norm_back_two = jax.vjp(layer_norm, stream_two, gain_two, shift_two)
    back_two, grad_gain_two, grad_shift_two = norm_back_two(grad_normed_two)
    grad_stream_two = grad_out.astype(jnp.float32) + back_two
    grad_attended = grad_stream_two.astype(jnp.bfloat16)
    grad_proj_weight = jnp.dot(mixed.T, grad_attended, preferred_element_type=jnp.float32)
    grad_proj_bias = column_sum(grad_attended)
    grad_mixed = jnp.dot(grad_attended, proj_weight.T, preferred_element_type=jnp.float32)
    grad_mixed = grad_mixed.astype(jnp.bfloat16).reshape(items, half, HEADS, HEAD_DIM)
    grad_probs = jnp.einsum(
        "iqhd,ikhd->ihqk", grad_mixed, value_heads, preferred_element_type=jnp.float32
    )
    grad_scores = probs * (grad_probs - jnp.sum(probs * grad_probs, axis=-1, keepdims=True))
    grad_scores = grad_scores.astype(jnp.bfloat16)
    grad_values = jnp.einsum(
        "ihqk,iqhd->ikhd", probs_low, grad_mixed, preferred_element_type=jnp.float32
    )
    grad_query = (
        jnp.einsum("ihqk,ikhd->iqhd", grad_scores, key_heads, preferred_element_type=jnp.float32)
        * scale
    )
    grad_keys = (
        jnp.einsum("ihqk,iqhd->ikhd", grad_scores, query_heads, preferred_element_type=jnp.float32)
        * scale
    )
    own_grad_keys, own_grad_values = (
        lax.psum_scatter(
            grad_keys.reshape(items, slots, width).astype(jnp.bfloat16),
            "seq",
            scatter_dimension=1,
            tiled=True,
        ).astype(jnp.float32),
        lax.psum_scatter(
            grad_values.reshape(items, slots, width).astype(jnp.bfloat16),
            "seq",
            scatter_dimension=1,
            tiled=True,
        ).astype(jnp.float32),
    )
    grad_packed = jnp.concatenate(
        [grad_query.reshape(items, half, width), own_grad_keys, own_grad_values], axis=-1
    )
    grad_packed = grad_packed.astype(jnp.bfloat16).reshape(rows, 3 * width)
    grad_qkv_weight = jnp.dot(normed.T, grad_packed, preferred_element_type=jnp.float32)
    grad_normed = jnp.dot(grad_packed, qkv_weight.T, preferred_element_type=jnp.float32)
    norm_out_one, norm_back_one = jax.vjp(layer_norm, stream, gain_one, shift_one)
    back_one, grad_gain_one, grad_shift_one = norm_back_one(grad_normed)
    grad_stream = (grad_stream_two + back_one).astype(jnp.bfloat16)
    grad_skip_weight = jnp.dot(joined.T, grad_stream, preferred_element_type=jnp.float32)
    grad_skip_bias = column_sum(grad_stream)
    grad_joined = jnp.dot(grad_stream, skip_weight.T, preferred_element_type=jnp.float32)
    grad_joined = grad_joined.reshape(items, half, 2 * width)
    grad_inputs = grad_joined[:, :, :width]
    own_grad_skip = grad_joined[:, :, width:]
    placed = lax.dynamic_update_slice_in_dim(
        jnp.zeros((items, slots, width), jnp.float32), own_grad_skip, first_slot, 1
    )
    grad_skipped = lax.psum_scatter(
        placed.astype(jnp.bfloat16), "seq", scatter_dimension=2, tiled=True
    ).astype(jnp.float32)
    dp_count = lax.axis_size("dp")

    def split_rows(values):
        share = values.shape[0] // (dp_count * seq_count)
        return values.reshape((dp_count, seq_count, share) + values.shape[1:])

    halved = (
        lax.psum_scatter(
            split_rows(grad_skip_weight).astype(jnp.bfloat16),
            "seq",
            scatter_dimension=1,
            tiled=True,
        ).astype(jnp.float32),
        lax.psum_scatter(
            split_rows(grad_skip_bias).astype(jnp.bfloat16), "seq", scatter_dimension=1, tiled=True
        ).astype(jnp.float32),
        lax.psum_scatter(
            split_rows(grad_gain_one).astype(jnp.bfloat16), "seq", scatter_dimension=1, tiled=True
        ).astype(jnp.float32),
        lax.psum_scatter(
            split_rows(grad_shift_one).astype(jnp.bfloat16), "seq", scatter_dimension=1, tiled=True
        ).astype(jnp.float32),
        lax.psum_scatter(
            split_rows(grad_qkv_weight).astype(jnp.bfloat16), "seq", scatter_dimension=1, tiled=True
        ).astype(jnp.float32),
        lax.psum_scatter(
            split_rows(grad_proj_weight).astype(jnp.bfloat16),
            "seq",
            scatter_dimension=1,
            tiled=True,
        ).astype(jnp.float32),
        lax.psum_scatter(
            split_rows(grad_proj_bias).astype(jnp.bfloat16), "seq", scatter_dimension=1, tiled=True
        ).astype(jnp.float32),
        lax.psum_scatter(
            split_rows(grad_gain_two).astype(jnp.bfloat16), "seq", scatter_dimension=1, tiled=True
        ).astype(jnp.float32),
        lax.psum_scatter(
            split_rows(grad_shift_two).astype(jnp.bfloat16), "seq", scatter_dimension=1, tiled=True
        ).astype(jnp.float32),
        lax.psum_scatter(
            split_rows(grad_fc1_weight).astype(jnp.bfloat16), "seq", scatter_dimension=1, tiled=True
        ).astype(jnp.float32),
        lax.psum_scatter(
            split_rows(grad_fc1_bias).astype(jnp.bfloat16), "seq", scatter_dimension=1, tiled=True
        ).astype(jnp.float32),
        lax.psum_scatter(
            split_rows(grad_fc2_weight).astype(jnp.bfloat16), "seq", scatter_dimension=1, tiled=True
        ).astype(jnp.float32),
        lax.psum_scatter(
            split_rows(grad_fc2_bias).astype(jnp.bfloat16), "seq", scatter_dimension=1, tiled=True
        ).astype(jnp.float32),
    )
    reduced = (
        lax.psum_scatter(halved[0], "dp", scatter_dimension=0, tiled=True),
        lax.psum_scatter(halved[1], "dp", scatter_dimension=0, tiled=True),
        lax.psum_scatter(halved[2], "dp", scatter_dimension=0, tiled=True),
        lax.psum_scatter(halved[3], "dp", scatter_dimension=0, tiled=True),
        lax.psum_scatter(halved[4], "dp", scatter_dimension=0, tiled=True),
        lax.psum_scatter(halved[5], "dp", scatter_dimension=0, tiled=True),
        lax.psum_scatter(halved[6], "dp", scatter_dimension=0, tiled=True),
        lax.psum_scatter(halved[7], "dp", scatter_dimension=0, tiled=True),
        lax.psum_scatter(halved[8], "dp", scatter_dimension=0, tiled=True),
        lax.psum_scatter(halved[9], "dp", scatter_dimension=0, tiled=True),
        lax.psum_scatter(halved[10], "dp", scatter_dimension=0, tiled=True),
        lax.psum_scatter(halved[11], "dp", scatter_dimension=0, tiled=True),
        lax.psum_scatter(halved[12], "dp", scatter_dimension=0, tiled=True),
    )
    summed = tuple((values.reshape(values.shape[2:]) for values in reduced))
    return (
        block_output,
        grad_inputs,
        grad_skipped,
        summed[0],
        summed[1],
        summed[2],
        summed[3],
        summed[4],
        summed[5],
        summed[6],
        summed[7],
        summed[8],
        summed[9],
        summed[10],
        summed[11],
        summed[12],
    )


def solution(mesh):
    return jax.shard_map(
        local,
        mesh=mesh,
        in_specs=(
            P("dp", "seq", None),
            P("dp", None, "seq"),
            P("dp"),
            P("dp", "seq", None),
            P(),
            P(),
            P(),
            P(),
            P(),
            P(),
            P(),
            P(),
            P(),
            P(),
            P(),
            P(),
            P(),
        ),
        out_specs=(
            P("dp", "seq", None),
            P("dp", "seq", None),
            P("dp", None, "seq"),
            P(("dp", "seq"), None),
            P(("dp", "seq")),
            P(("dp", "seq")),
            P(("dp", "seq")),
            P(("dp", "seq"), None),
            P(("dp", "seq"), None),
            P(("dp", "seq")),
            P(("dp", "seq")),
            P(("dp", "seq")),
            P(("dp", "seq"), None),
            P(("dp", "seq")),
            P(("dp", "seq"), None),
            P(("dp", "seq")),
        ),
        check_vma=False,
    )
```

profile of v0, /device:TPU:0, one launch (start us, length us, event | category | flops | bytes accessed | tf_op | source)
XLA Modules:
  0.0 1601.1 jit_solution(12497732356068369279)
XLA Ops:
  10.6 32.2 %all-gather.4.cloned.1.call-done = bf16[2,336,1152]{1,0,2:T(2,128)(2,1)} async-done(((bf16[2,336,576]{1,0,2:T(2,128)(2,1)}), bf16[2,336,1152]{1,0,2:T(2,128)(2,1)}) %all-gather.4.cloned.1.call-update) | async-done | bytes 1548304 | tf_op jit(solution)/shard_map/all_gather | solution.py:54
  65.9 24.6 %all-gather.8.cloned.1.call-done = bf16[2,336,1152]{2,1,0:T(8,128)(2,1)} async-done(((bf16[2,168,1152]{2,1,0:T(8,128)(2,1)}), bf16[2,336,1152]{2,1,0:T(8,128)(2,1)}) %all-gather.8.cloned.1.call-update) | async-done | bytes 1548304 | tf_op jit(solution)/shard_map/all_gather | solution.py:66
  102.5 17.1 %all-gather.6.cloned.1.call-done = bf16[2,336,1152]{2,1,0:T(8,128)(2,1)} async-done(((bf16[2,168,1152]{2,1,0:T(8,128)(2,1)}), bf16[2,336,1152]{2,1,0:T(8,128)(2,1)}) %all-gather.6.cloned.1.call-update) | async-done | bytes 1548304 | tf_op jit(solution)/shard_map/all_gather | solution.py:67
  138.4 21.1 %fusion.5 = (bf16[4608,336]{0,1:T(8,128)(2,1)}, f32[336,4608]{1,0:T(8,128)S(1)}) fusion(f32[4608]{0:T(1024)S(1)} %copy-done.38, bf16[1152,4608]{1,0:T(8,128)(2,1)} %param.30, f32[336,1152]{1,0:T(8,128)S(1)} %get-tuple-element.57, f32[1152]{0:T(1024)S(1)} %copy-done.40, f32[1152]{0:T(1024)S(1)} %copy-done.34, f32[336]{0:T(512)S(1)} %fusion.57, ...), kind=kOutput, calls=%fused_computation.15 | convolution fusion | flops 3671377920 | bytes 21485184 | tf_op jit(solution)/shard_map/dot_general | solution.py:93
  159.5 20.4 %fusion.71 = (bf16[4608]{0:T(1024)(128)(2,1)S(1)}, bf16[336,4608]{1,0:T(8,128)(2,1)}, f32[336,4608]{1,0:T(8,128)}) fusion(f32[336,4608]{1,0:T(8,128)S(1)} %get-tuple-element.63, bf16[336,1152]{1,0:T(8,128)(2,1)S(1)} %bitcast.196, bf16[4608,1152]{1,0:T(8,128)(2,1)S(1)} %bitcast.230), kind=kOutput, calls=%fused_computation.144 | convolution fusion | flops 3680275968 | bytes 26883072 | tf_op jit(solution)/shard_map/dot_general | solution.py:103
  249.0 66.7 %all-reduce.29.cloned.1.call-done = (bf16[2,336,1152]{2,0,1:T(2,128)(2,1)}, bf16[2,336,1152]{2,0,1:T(2,128)(2,1)}) async-done(((bf16[2,336,1152]{2,0,1:T(2,128)(2,1)}, bf16[2,336,1152]{2,0,1:T(2,128)(2,1)}), (bf16[2,336,1152]{2,0,1:T(2,128)(2,1)}, bf16[2,336,1152]{2,0,1:T(2,128)(2,1)})) %all-reduce.29.cloned.1.call-update) | async-done | bytes 3096592
  355.7 10.9 convolution_convert_fusion.1
  397.3 10.5 convolution_convert_fusion
  407.8 14.2 convert_element_type.224
  422.0 12.3 copy.159
  439.2 13.4 reduce-scatter.30.cloned.1.call-done
  461.5 354.4 %all-reduce.27.cloned.1.call-done = (bf16[16,2,72,1152]{3,2,1,0:T(8,128)(2,1)}, bf16[16,2,144,1152]{3,2,1,0:T(8,128)(2,1)}) async-done(((bf16[16,2,72,1152]{3,2,1,0:T(8,128)(2,1)}, bf16[16,2,144,1152]{3,2,1,0:T(8,128)(2,1)}), (bf16[16,2,72,1152]{3,2,1,0:T(8,128)(2,1)}, bf16[16,2,144,1152]{3,2,1,0:T(8,128)(2,1)})) %all-reduce.27.cloned.1.call-update) | async-done | bytes 15925264
  831.0 12.6 fusion.33
  844.3 9.0 reduce-scatter.36.cloned.1.call-done
  854.0 11.3 reduce-scatter.38.cloned.1.call-done
  866.0 11.8 reduce-scatter.42.cloned.1.call-done
  881.2 9.3 reduce-scatter.24.cloned.1.call-done
  891.1 11.8 reduce-scatter.26.cloned.1.call-done
  903.6 11.2 reduce-scatter.28.cloned.1.call-done
  915.4 29.8 %reduce-scatter.48.cloned.1.call-done = bf16[576,672]{1,0:T(8,128)(2,1)} async-done(((bf16[1152,672]{1,0:T(8,128)(2,1)}), bf16[576,672]{1,0:T(8,128)(2,1)}) %reduce-scatter.48.cloned.1.call-update) | async-done | bytes 774160
  950.7 120.0 %reduce-scatter.40.cloned.1.call-done = bf16[16,1,36,4608]{3,0,2,1:T(8,128)(2,1)} async-done(((bf16[16,2,36,4608]{3,0,2,1:T(8,128)(2,1)}), bf16[16,1,36,4608]{3,0,2,1:T(8,128)(2,1)}) %reduce-scatter.40.cloned.1.call-update) | async-done | bytes 5308432 | tf_op jit(solution)/shard_map/reduce_scatter | solution.py:207
  1070.7 307.8 %all-reduce.30 = (f32[16,1,36]{2,1,0:T(1,128)S(1)}, f32[16,1,36]{2,1,0:T(1,128)S(1)}, f32[16,1,36]{2,1,0:T(1,128)S(1)}, f32[16,1,36]{2,1,0:T(1,128)S(1)}, f32[16...) all-reduce(f32[16,1,36]{2,1,0:T(1,128)S(1)} %bitcast.223, ...), channel_id=8, replica_groups=mesh['dp'=16,'seq'=2] {'dp'}, use_global_device_ids=true, to_apply=%region_18.19.clone | all-reduce | flops 2660544 | bytes 15975936
  1396.5 73.5 %reduce-scatter.50.cloned.1.call-done = f32[1,1,72,1152]{3,2,1,0:T(8,128)} async-done(((f32[16,1,72,1152]{3,2,1,0:T(8,128)}), f32[1,1,72,1152]{3,2,1,0:T(8,128)}) %reduce-scatter.50.cloned.1.call-update) | async-done | bytes 331792
  1469.9 123.8 %reduce-scatter.44.cloned.1.call-done = f32[1,1,144,1152]{3,2,1,0:T(8,128)} async-done(((f32[16,1,144,1152]{3,2,1,0:T(8,128)}), f32[1,1,144,1152]{3,2,1,0:T(8,128)}) %reduce-scatter.44.cloned.1.call-update) | async-done | bytes 663568 | tf_op jit(solution)/shard_map/reduce_scatter | solution.py:232
  (269 shorter events, 255.2 us)
Async XLA Ops:
  7.2 127.5 %copy-start = (bf16[1152,1152]{1,0:T(8,128)(2,1)S(1)}, bf16[1152,1152]{1,0:T(8,128)(2,1)}, u32[]{:S(2)}) copy-start(bf16[1152,1152]{1,0:T(8,128)(2,1)} %param.26) | copy-start | bytes 7962628
  7.2 35.7 %all-gather.4.cloned.1.call-start = ((), (), s32[]{:S(2)}) async-start(), calls=%async_computation.14 | async-start | bytes 2654208 | tf_op jit(solution)/shard_map/all_gather | solution.py:54
  10.6 79.9 %all-gather.8.cloned.1.call-start = ((), (), s32[]{:S(2)}) async-start(), calls=%async_computation.16 | async-start | bytes 2322432 | tf_op jit(solution)/shard_map/all_gather | solution.py:66
  63.4 56.2 %all-gather.6.cloned.1.call-start = ((), (), s32[]{:S(2)}) async-start(), calls=%async_computation.15 | async-start | bytes 2322432 | tf_op jit(solution)/shard_map/all_gather | solution.py:67
  64.2 251.5 %all-reduce.29.cloned.1.call-start = ((), (), s32[]{:S(2)}) async-start(), calls=%async_computation.33 | async-start | bytes 6193152
  230.6 203.7 %reduce-scatter.32.cloned.1.call-start = ((), (), s32[]{:S(2)}) async-start(), calls=%async_computation.21 | async-start | bytes 3981312 | tf_op jit(solution)/shard_map/reduce_scatter | solution.py:192
  236.0 216.7 %reduce-scatter.30.cloned.1.call-start = ((), (), s32[]{:S(2)}) async-start(), calls=%async_computation.20 | async-start | bytes 11943936 | tf_op jit(solution)/shard_map/reduce_scatter | solution.py:189
  242.6 77.0 %copy-start.33 = (f32[1152]{0:T(1024)S(1)}, f32[1152]{0:T(1024)}, u32[]{:S(2)}) copy-start(f32[1152]{0:T(1024)} %param.23) | copy-start | bytes 13828
  242.6 77.0 %copy-start.36 = (f32[336]{0:T(512)S(1)}, f32[336]{0:T(512)}, u32[]{:S(2)}) copy-start(f32[336]{0:T(512)} %copy-done.35) | copy-start | bytes 4036
  346.5 469.3 %all-reduce.27.cloned.1.call-start = ((), (), s32[]{:S(2)}) async-start(), calls=%async_computation.32 | async-start | bytes 31850496
  372.0 458.3 %reduce-scatter.46.cloned.1.call-start = ((), (), s32[]{:S(2)}) async-start(), calls=%async_computation.28 | async-start | bytes 12288 | tf_op jit(solution)/shard_map/reduce_scatter | solution.py:216
  373.0 470.7 %reduce-scatter.34.cloned.1.call-start = ((), (), s32[]{:S(2)}) async-start(), calls=%async_computation.22 | async-start | bytes 12288 | tf_op jit(solution)/shard_map/reduce_scatter | solution.py:198
  373.8 479.6 %reduce-scatter.36.cloned.1.call-start = ((), (), s32[]{:S(2)}) async-start(), calls=%async_computation.23 | async-start | bytes 12288 | tf_op jit(solution)/shard_map/reduce_scatter | solution.py:201
  374.6 490.8 %reduce-scatter.38.cloned.1.call-start = ((), (), s32[]{:S(2)}) async-start(), calls=%async_computation.24 | async-start | bytes 12288 | tf_op jit(solution)/shard_map/reduce_scatter | solution.py:204
  375.4 502.5 %reduce-scatter.42.cloned.1.call-start = ((), (), s32[]{:S(2)}) async-start(), calls=%async_computation.26 | async-start | bytes 24576 | tf_op jit(solution)/shard_map/reduce_scatter | solution.py:210
  376.2 514.3 %reduce-scatter.24.cloned.1.call-start = ((), (), s32[]{:S(2)}) async-start(), calls=%async_computation.17 | async-start | bytes 12288 | tf_op jit(solution)/shard_map/reduce_scatter | solution.py:180
  376.9 525.9 %reduce-scatter.26.cloned.1.call-start = ((), (), s32[]{:S(2)}) async-start(), calls=%async_computation.18 | async-start | bytes 12288 | tf_op jit(solution)/shard_map/reduce_scatter | solution.py:183
  377.7 537.0 %reduce-scatter.28.cloned.1.call-start = ((), (), s32[]{:S(2)}) async-start(), calls=%async_computation.19 | async-start | bytes 12288 | tf_op jit(solution)/shard_map/reduce_scatter | solution.py:186
  385.1 560.1 %reduce-scatter.48.cloned.1.call-start = ((), (), s32[]{:S(2)}) async-start(), calls=%async_computation.29 | async-start | bytes 2654208
  397.0 673.7 %reduce-scatter.40.cloned.1.call-start = ((), (), s32[]{:S(2)}) async-start(), calls=%async_computation.25 | async-start | bytes 15925248 | tf_op jit(solution)/shard_map/reduce_scatter | solution.py:207
  434.3 957.4 %all-reduce.25.cloned.1.call-start = ((), (), s32[]{:S(2)}) async-start(), calls=%async_computation.31 | async-start | bytes 21233664
  461.4 1008.5 %reduce-scatter.50.cloned.1.call-start = ((), (), s32[]{:S(2)}) async-start(), calls=%async_computation.30 | async-start | bytes 5640192
  821.0 772.8 %reduce-scatter.44.cloned.1.call-start = ((), (), s32[]{:S(2)}) async-start(), calls=%async_computation.27 | async-start | bytes 11280384 | tf_op jit(solution)/shard_map/reduce_scatter | solution.py:232
  1070.7 523.1 %copy-start.1 = (bf16[1152,1152]{1,0:T(8,128)(2,1)S(1)}, bf16[1152,1152]{1,0:T(8,128)(2,1)}, u32[]{:S(2)}) copy-start(bf16[1152,1152]{1,0:T(8,128)(2,1)} %param.26) | copy-start | bytes 7962628
  (50 other events, 682.0 us)
Sparse Core Ops, SparseCore 0:
  10.7 32.1 all-gather.3
  63.6 26.9 all-gather.7
  92.6 26.9 all-gather.5
  230.7 84.8 all-reduce.28
  317.8 37.9 reduce-scatter.31
  357.9 94.6 reduce-scatter.29
  455.3 360.5 all-reduce.26
  818.7 10.7 reduce-scatter.45
  831.7 9.7 reduce-scatter.33
  843.6 9.6 reduce-scatter.35
  855.6 9.7 reduce-scatter.37
  868.1 9.7 reduce-scatter.41
  880.7 9.7 reduce-scatter.23
  893.1 9.7 reduce-scatter.25
  905.0 9.7 reduce-scatter.27
  917.0 28.2 reduce-scatter.47
  947.4 123.2 reduce-scatter.39
  1074.8 311.1 all-reduce.24
  1390.6 79.3 reduce-scatter.49
  1474.4 119.2 reduce-scatter.43
where the time goes:
time: 1610 us; the launch traced here: 1600 us
  waiting for transfers between devices  921 us (57%)
  blocking collectives  308 us (19%)
  local copies, waits for them, and re-layouts  163 us (10%)
  matrix products  160 us (10%)
  other arithmetic  31.1 us (2%)
  between operations  16.3 us (1%)
    unnamed x25, waiting for transfers between devices  525 us
    unnamed x1, blocking collectives  308 us
    reduce_scatter x1, waiting for transfers between devices, local(): lax.psum_scatter(halved[11], 'dp', scatter_dimension=0, tiled=True)  124 us
    reduce_scatter x1, waiting for transfers between devices, local(): lax.psum_scatter(split_rows(grad_fc1_weight).astype(jnp.bfloat16), 'seq',...  120 us
    unnamed x125, local copies, waits for them, and re-layouts  41.2 us
    all_gather x1, waiting for transfers between devices, local(): whole_skip = lax.all_gather(skipped, 'seq', axis=2, tiled=True)  32.2 us
  transfers between devices with their start and end apart: 20, of which 16 were waited for; matrix products, arithmetic and copies ran while one was open for 14% of the time, Pallas kernels for 0%

commit v1 on v0

v1 whole, which is shorter than its diff:
```python
import jax
import jax.numpy as jnp
from jax import lax
from jax.sharding import PartitionSpec as P

HEADS = 16
HEAD_DIM = 72
CAPTION = 77
IMAGE = 256


epsilon = 1e-05
masked_score = -1e30


def layer_norm(stream, gain, shift):
    center = stream - jnp.mean(stream, axis=-1, keepdims=True)
    spread = jnp.mean(center * center, axis=-1, keepdims=True)
    return center * lax.rsqrt(spread + epsilon) * gain + shift


def gelu_exact(values):
    return jax.nn.gelu(values, approximate=False)


def column_sum(values):
    return jnp.sum(values.astype(jnp.float32), axis=0)


def matmul(left, right):
    return jnp.dot(left, right, preferred_element_type=jnp.float32)


def swap_seq(values):
    return lax.ppermute(values, "seq", [(0, 1), (1, 0)])


def swap_dp(values, bit):
    count = lax.axis_size("dp")
    return lax.ppermute(values, "dp", [(i, i ^ (1 << bit)) for i in range(count)])


def pick(values, index, axis):
    return lax.dynamic_index_in_dim(values, index, axis, keepdims=False)


def place(first, own, got, axis):
    return jnp.where(
        first, jnp.concatenate([own, got], axis=axis), jnp.concatenate([got, own], axis=axis)
    )


def halving(block, order, bits):
    dp_index = lax.axis_index("dp")
    seq_index = lax.axis_index("seq")
    dims = list(reversed(range(1, bits))) + ["seq"]
    for name in order:
        axis = dims.index(name)
        own = seq_index if name == "seq" else (dp_index >> name) & 1
        sent = pick(block, 1 - own, axis)
        kept = pick(block, own, axis)
        got = swap_seq(sent) if name == "seq" else swap_dp(sent, name)
        total = kept.astype(jnp.float32) + got.astype(jnp.float32)
        dims.pop(axis)
        block = total.astype(jnp.bfloat16) if dims else total
    return block


def local(
    inputs,
    skipped,
    lengths,
    cotangent,
    skip_weight,
    skip_bias,
    gain_one,
    shift_one,
    qkv_weight,
    proj_weight,
    proj_bias,
    gain_two,
    shift_two,
    fc1_weight,
    fc1_bias,
    fc2_weight,
    fc2_bias,
):
    items, half, width = inputs.shape
    seq_count = lax.axis_size("seq")
    dp_count = lax.axis_size("dp")
    bits = dp_count.bit_length() - 1
    seq_index = lax.axis_index("seq")
    core = lax.axis_index("dp") & 1
    first = seq_index == 0
    slots = half * seq_count

    def whole_item(values, axis):
        own = pick(values, seq_index, 0)
        got = swap_seq(pick(values, 1 - seq_index, 0))
        return place(first, own, got, axis)

    def to_owner(values, axis):
        parts = jnp.split(values, 2, axis=axis)
        own = jnp.where(first, parts[0], parts[1])
        other = jnp.where(first, parts[1], parts[0])
        got = swap_seq(other.astype(jnp.bfloat16)).astype(values.dtype)
        return place(first, own[None], got[None], 0)

    own_inputs = whole_item(inputs, 0)
    own_skip = whole_item(skipped, 1)
    grad_out = whole_item(cotangent, 0)
    length = pick(lengths, seq_index, 0)
    rows = slots

    joined = jnp.concatenate([own_inputs, own_skip], axis=-1)
    stream = matmul(joined, skip_weight) + skip_bias
    normed = layer_norm(stream, gain_one, shift_one).astype(jnp.bfloat16)
    packed = matmul(normed, qkv_weight).astype(jnp.bfloat16)
    heads = packed.reshape(rows, 3, HEADS, HEAD_DIM)
    query, keys, values = heads[:, 0], heads[:, 1], heads[:, 2]
    scale = HEAD_DIM ** (-0.5)
    positions = jnp.arange(slots, dtype=jnp.int32)
    caption = (positions >= 1) & (positions <= length)
    image = (positions >= 1 + CAPTION) & (positions < 1 + CAPTION + IMAGE)
    valid = (positions == 0) | caption | image

    def product(spec, left, right):
        return jnp.einsum(spec, left, right, preferred_element_type=jnp.float32)

    scores = product("qhd,khd->hqk", query, keys) * scale
    scores = jnp.where(valid[None, None, :], scores, masked_score)
    top = jnp.max(scores, axis=-1, keepdims=True)
    expo = jnp.exp(scores - top)
    probs = expo / jnp.sum(expo, axis=-1, keepdims=True)
    probs_low = probs.astype(jnp.bfloat16)
    mixed = product("hqk,khd->qhd", probs_low, values)
    mixed = mixed.astype(jnp.bfloat16).reshape(rows, width)
    attended = matmul(mixed, proj_weight) + proj_bias
    stream_two = stream + attended
    normed_two = layer_norm(stream_two, gain_two, shift_two).astype(jnp.bfloat16)
    hidden = matmul(normed_two, fc1_weight) + fc1_bias
    acted, gelu_back = jax.vjp(gelu_exact, hidden)
    acted_low = acted.astype(jnp.bfloat16)
    block_output = (stream_two + (matmul(acted_low, fc2_weight) + fc2_bias)).astype(jnp.bfloat16)

    blocks = dp_count // 2

    def own_rows(left, right):
        parts = left.reshape(rows, blocks, 2, -1)
        kept = pick(parts, core, 2).reshape(rows, -1)
        sent = pick(parts, 1 - core, 2).reshape(rows, -1)
        left_both = jnp.concatenate([kept, swap_dp(sent, 0)], axis=0)
        right_both = jnp.concatenate([right, swap_dp(right, 0)], axis=0)
        total = matmul(left_both.T, right_both).astype(jnp.bfloat16)
        share = total.shape[0] // (blocks * 2)
        return total.reshape((2,) * bits + (share, right.shape[1]))

    above = list(range(1, bits))
    order_x = ["seq"] + above
    order_y = above + ["seq"]
    order_z = above[1:] + ["seq"] + above[:1]

    grad_fc2 = halving(own_rows(acted_low, grad_out), order_x, bits)
    grad_fc2_bias = column_sum(grad_out)
    grad_acted = matmul(grad_out, fc2_weight.T)
    grad_hidden = gelu_back(grad_acted)[0].astype(jnp.bfloat16)
    grad_fc1 = halving(own_rows(normed_two, grad_hidden), order_x, bits)
    grad_fc1_bias = column_sum(grad_hidden)
    grad_normed_two = matmul(grad_hidden, fc1_weight.T)
    _, norm_back_two = jax.vjp(layer_norm, stream_two, gain_two, shift_two)
    back_two, grad_gain_two, grad_shift_two = norm_back_two(grad_normed_two)
    grad_stream_two = grad_out.astype(jnp.float32) + back_two
    grad_attended = grad_stream_two.astype(jnp.bfloat16)
    grad_proj = halving(own_rows(mixed, grad_attended), order_y, bits)
    grad_proj_bias = column_sum(grad_attended)
    grad_mixed = matmul(grad_attended, proj_weight.T)
    grad_mixed = grad_mixed.astype(jnp.bfloat16).reshape(rows, HEADS, HEAD_DIM)
    grad_probs = product("qhd,khd->hqk", grad_mixed, values)
    grad_scores = probs * (grad_probs - jnp.sum(probs * grad_probs, axis=-1, keepdims=True))
    grad_scores = grad_scores.astype(jnp.bfloat16)
    grad_values = product("hqk,qhd->khd", probs_low, grad_mixed)
    grad_query = product("hqk,khd->qhd", grad_scores, keys) * scale
    grad_keys = product("hqk,qhd->khd", grad_scores, query) * scale
    grad_packed = jnp.stack([grad_query, grad_keys, grad_values], axis=1)
    grad_packed = grad_packed.astype(jnp.bfloat16).reshape(rows, 3 * width)
    grad_qkv = halving(own_rows(normed, grad_packed), order_y, bits)
    grad_normed = matmul(grad_packed, qkv_weight.T)
    _, norm_back_one = jax.vjp(layer_norm, stream, gain_one, shift_one)
    back_one, grad_gain_one, grad_shift_one = norm_back_one(grad_normed)
    grad_stream = (grad_stream_two + back_one).astype(jnp.bfloat16)
    grad_skip = halving(own_rows(joined, grad_stream), order_z, bits)
    grad_skip_bias = column_sum(grad_stream)
    grad_joined = matmul(grad_stream, skip_weight.T)

    vectors = (
        grad_skip_bias,
        grad_gain_one,
        grad_shift_one,
        grad_proj_bias,
        grad_gain_two,
        grad_shift_two,
        grad_fc1_bias,
        grad_fc2_bias,
    )
    chunks = dp_count * seq_count
    line = jnp.concatenate([v.reshape(chunks, -1) for v in vectors], axis=1)
    line = lax.psum_scatter(line, ("dp", "seq"), scatter_dimension=0, tiled=True)[0]
    pieces, start = [], 0
    for vector in vectors:
        size = vector.shape[0] // chunks
        pieces.append(line[start : start + size])
        start += size

    return (
        to_owner(block_output, 0),
        to_owner(grad_joined[:, :width], 0),
        to_owner(grad_joined[:, width:], 1),
        grad_skip,
        pieces[0],
        pieces[1],
        pieces[2],
        grad_qkv,
        grad_proj,
        pieces[3],
        pieces[4],
        pieces[5],
        grad_fc1,
        pieces[6],
        grad_fc2,
        pieces[7],
    )


def solution(mesh):
    return jax.shard_map(
        local,
        mesh=mesh,
        in_specs=(
            P("dp", "seq", None),
            P("dp", None, "seq"),
            P("dp"),
            P("dp", "seq", None),
        )
        + (P(),) * 13,
        out_specs=(
            P("dp", "seq", None),
            P("dp", "seq", None),
            P("dp", None, "seq"),
            P(("dp", "seq"), None),
            P(("dp", "seq")),
            P(("dp", "seq")),
            P(("dp", "seq")),
            P(("dp", "seq"), None),
            P(("dp", "seq"), None),
            P(("dp", "seq")),
            P(("dp", "seq")),
            P(("dp", "seq")),
            P(("dp", "seq"), None),
            P(("dp", "seq")),
            P(("dp", "seq"), None),
            P(("dp", "seq")),
        ),
        check_vma=False,
    )
```

time: 1610 us -> 576 us (0.36)
  waiting for transfers between devices: 921 us -> 183 us
  blocking collectives: 308 us -> 41.8 us
  local copies, waits for them, and re-layouts: 163 us -> 108 us
  starting transfers between devices: 1.93 us -> 41.2 us
  other arithmetic: 31.1 us -> 70 us
  matrix products: 160 us -> 123 us
    unnamed x25 -> x0, waiting for transfers between devices: 525 us -> none
    reduce_scatter x12 -> x0, waiting for transfers between devices: 322 us -> none  [the longest x1 124 us: local(): lax.psum_scatter(halved[11], 'dp', scatter_dimension=0, tiled=True)]
    unnamed x1, blocking collectives: 308 us -> 41.8 us
    ppermute x0 -> x36, waiting for transfers between devices: none -> 183 us  [the longest x25 122 us: swap_dp(): return lax.ppermute(values, 'dp', [(i, i ^ 1 << bit) for i in range(count)])]
    all_gather x3 -> x0, waiting for transfers between devices: 74 us -> none  [the longest x1 32.2 us: local(): whole_skip = lax.all_gather(skipped, 'seq', axis=2, tiled=True)]
    convert_element_type x26 -> x4, local copies, waits for them, and re-layouts: 69.9 us -> 11.6 us  [the longest x1 4.89 us: local(): packed = matmul(normed, qkv_weight).astype(jnp.bfloat16)]
    ppermute x0 -> x36, starting transfers between devices: none -> 41.2 us  [the longest x25 28.6 us: swap_dp(): return lax.ppermute(values, 'dp', [(i, i ^ 1 << bit) for i in range(count)])]
    dynamic_slice x1 -> x26, local copies, waits for them, and re-layouts: 3.86 us -> 39.1 us  [pick(): return lax.dynamic_index_in_dim(values, index, axis, keepdims=False)]
  transfers between devices with their start and end apart: 20 -> 36, of which waited for: 16 -> 17; matrix products, arithmetic and copies ran while one was open for 14% -> 51% of each run, Pallas kernels for 0% -> 0%
where the time goes in v1:
time: 576 us; the launch traced here: 569 us
  waiting for transfers between devices  183 us (32%)
  matrix products  123 us (21%)
  local copies, waits for them, and re-layouts  108 us (19%)
  other arithmetic  70 us (12%)
  blocking collectives  41.8 us (7%)
  starting transfers between devices  41.2 us (7%)
    ppermute x25, waiting for transfers between devices, swap_dp(): return lax.ppermute(values, 'dp', [(i, i ^ 1 << bit) for i in range(count)])  122 us
    dot_general x15, matrix products, matmul(): return jnp.dot(left, right, preferred_element_type=jnp.float32)  106 us
    ppermute x11, waiting for transfers between devices, swap_seq(): return lax.ppermute(values, 'seq', [(0, 1), (1, 0)])  61.1 us
    unnamed x1, blocking collectives  41.8 us
    dynamic_slice x26, local copies, waits for them, and re-layouts, pick(): return lax.dynamic_index_in_dim(values, index, axis, keepdims=False)  39.1 us
    ppermute x25, starting transfers between devices, swap_dp(): return lax.ppermute(values, 'dp', [(i, i ^ 1 << bit) for i in range(count)])  28.6 us
    select_n x7, other arithmetic, place(): jnp.where(first, jnp.concatenate([own, got], axis=axis), jnp.concatenate(...  19.9 us
    reshape x3, local copies, waits for them, and re-layouts, own_rows(): return total.reshape((2,) * bits + (share, right.shape[1]))  16.9 us
  transfers between devices with their start and end apart: 36, of which 17 were waited for; matrix products, arithmetic and copies ran while one was open for 51% of the time, Pallas kernels for 0%

profile of v1, /device:TPU:0, one launch (start us, length us, event | category | flops | bytes accessed | tf_op | source)
XLA Modules:
  0.0 569.1 jit_solution(9946411242509230132)
XLA Ops:
  18.9 6.1 %collective-permute-done.1 = bf16[336,576]{1,0:T(8,128)(2,1)} collective-permute-done((bf16[336,576]{1,0:T(8,128)(2,1)}, bf16[336,576]{1,0:T(8,128)(2,1)}, u32[]{:S(2)}, u32[]{:S(2)}) %collective-permute-start.1) | collective-permute-done | bytes 387104 | tf_op jit(solution)/shard_map/ppermute | solution.py:35
  60.4 7.0 %convolution_add_fusion = f32[336,4608]{1,0:T(8,128)S(1)} fusion(bf16[336,1152]{1,0:T(8,128)(2,1)S(1)} %add_convert_fusion.2, bf16[1152,4608]{1,0:T(8,128)(2,1)} %param.30, f32[4608]{0:T(1024)S(1)} %copy-done.46), kind=kOutput, calls=%fused_computation.9 | convolution fusion | flops 3568803840 | bytes 17602560 | tf_op jit(solution)/shard_map/dot_general | solution.py:31
  67.5 23.8 %convert_reduce_fusion = (f32[4608]{0:T(1024)}, bf16[336,4608]{1,0:T(8,128)(2,1)}, f32[336,4608]{1,0:T(8,128)}) fusion(f32[336,4608]{1,0:T(8,128)S(1)} %convolution_add_fusion, bf16[336,1152]{1,0:T(8,128)(2,1)} %get-tuple-element.23, bf16[4608,1152]{1,0:T(8,128)(2,1)} %param.32), kind=kOutput, calls=%fused_computation.15 | convolution fusion | flops 3681824256 | bytes 26892288 | tf_op jit(solution)/shard_map/dot_general | solution.py:31
  91.3 6.9 %multiply_reduce_fusion.1 = (f32[1152]{0:T(1024)}, f32[336]{0:T(512)S(1)}, f32[1152]{0:T(1024)}, f32[336,1152]{1,0:T(8,128)S(1)}) fusion(f32[336,1152]{1,0:T(8,128)S(1)} %copy-done.4, f32[336]{0:T(512)S(1)} %fusion.85, f32[336]{0:T(512)S(1)} %broadcast_multiply_fusion, f32[1152]{0:T(1024)S(1)} %copy-done.32, bf16[336,4608]{1,0:T(8,128)(2,1)} %get-tuple-element.25, ...), kind=kOutput, calls=%fused_computation.101 | convolution fusion | flops 3570349568 | bytes 16827840 | tf_op jit(solution)/shard_map/dot_general | solution.py:31
  128.9 8.7 %multiply_reduce_fusion.2 = (f32[1152]{0:T(1024)}, f32[336]{0:T(512)S(1)}, f32[1152]{0:T(1024)}, f32[336,1152]{1,0:T(8,128)S(1)}) fusion(f32[336,1152]{1,0:T(8,128)S(1)} %copy-done.8, f32[336]{0:T(512)S(1)} %fusion.84, f32[336]{0:T(512)S(1)} %broadcast_multiply_fusion.1, f32[1152]{0:T(1024)S(1)} %copy-done.33, bf16[336,3456]{0,1:T(8,128)(2,1)} %bitcast.237, ...), kind=kOutput, calls=%fused_computation.103 | convolution fusion | flops 2678535680 | bytes 13399488 | tf_op jit(solution)/shard_map/dot_general | solution.py:31
  168.8 41.8 %all-reduce = f32[32,396]{1,0:T(8,128)S(1)} all-reduce(f32[32,396]{1,0:T(8,128)S(1)} %concatenate.119), channel_id=2, replica_groups=mesh['dp'=16,'seq'=2] {'dp','seq'}, use_global_device_ids=true, to_apply=%region_19.20.clone | all-reduce | flops 12672 | bytes 101376
  221.3 8.2 %broadcast_select_fusion.1 = bf16[336,4,2,144]{3,2,1,0:T(2,128)(2,1)S(1)} fusion(pred[]{:T(512)S(6)} %eq.13, bf16[168,4,2,144]{3,2,1,0:T(2,128)(2,1)} %concatenate.109, bf16[168,4,2,144]{3,2,1,0:T(2,128)(2,1)S(1)} %copy-done.21), kind=kLoop, calls=%fused_computation.60 | loop fusion | flops 1161216 | bytes 1548289 | tf_op jit(solution)/shard_map/jit(_where)/select_n | solution.py:48
  229.5 9.6 %dynamic-slice_maximum_fusion.1 = (bf16[336,8,1,144]{3,2,1,0:T(2,128)(2,1)}, bf16[336,8,1,144]{3,2,1,0:T(2,128)(2,1)}) fusion(s32[]{:T(128)S(6)} %select_n.210, bf16[336,4,2,144]{3,2,1,0:T(2,128)(2,1)S(1)} %broadcast_select_fusion, bf16[336,4,2,144]{3,2,1,0:T(2,128)(2,1)S(1)} %broadcast_select_fusion.1, s32[]{:T(128)S(6)} %select_n.211), kind=kLoop, calls=%fused_computation.58 | loop fusion | flops 3096576 | bytes 3096584 | tf_op jit(solution)/shard_map/concatenate | solution.py:115
  253.9 9.1 %fusion.26 = bf16[336,1152]{1,0:T(8,128)(2,1)S(1)} fusion(f32[336,1152]{1,0:T(8,128)S(1)} %copy-done.5, bf16[336,4608]{1,0:T(8,128)(2,1)} %multiply_convert_fusion.1, bf16[4608,1152]{1,0:T(8,128)(2,1)} %param.32, f32[1152]{0:T(1024)S(1)} %copy-done.49), kind=kOutput, calls=%fused_computation.62 | convolution fusion | flops 3568416768 | bytes 16040448 | tf_op jit(solution)/shard_map/dot_general | solution.py:31
  265.7 8.6 %collective-permute-done.2 = bf16[168,1152]{1,0:T(8,128)(2,1)S(1)} collective-permute-done((bf16[168,1152]{1,0:T(8,128)(2,1)S(1)}, bf16[168,1152]{1,0:T(8,128)(2,1)S(1)}, u32[]{:S(2)}, u32[]{:S(2)}) %collective-permute-start.2) | collective-permute-done | bytes 387104 | tf_op jit(solution)/shard_map/ppermute | solution.py:35
  319.5 7.3 %convolution_convert_fusion = bf16[2304,1152]{1,0:T(8,128)(2,1)S(1)} fusion(bf16[336,2304]{0,1:T(8,128)(2,1)} %copy.148, bf16[336,2304]{0,1:T(8,128)(2,1)} %bitcast.255, bf16[336,1152]{1,0:T(8,128)(2,1)} %collective-permute-done.31, bf16[336,1152]{1,0:T(8,128)(2,1)} %get-tuple-element.23), kind=kOutput, calls=%fused_computation.1 | convolution fusion | flops 3579199488 | bytes 9953280 | tf_op jit(solution)/shard_map/dot_general | solution.py:31
  326.8 22.7 %collective-permute-done.22 = bf16[2,36,1152]{2,1,0:T(8,128)(2,1)S(1)} collective-permute-done((bf16[2,36,1152]{2,1,0:T(8,128)(2,1)S(1)}, bf16[2,36,1152]{2,1,0:T(8,128)(2,1)S(1)}, u32[]{:S(2)}, u32[]{:S(2)}) %collective-permute-start.22) | collective-permute-done | bytes 165920 | tf_op jit(solution)/shard_map/ppermute | solution.py:40
  360.5 7.7 %convolution_convert_fusion.3 = bf16[576,3456]{1,0:T(8,128)(2,1)} fusion(bf16[336,3456]{1,0:T(8,128)(2,1)} %collective-permute-done.13, bf16[336,3456]{1,0:T(8,128)(2,1)} %copy.130, bf16[336,576]{0,1:T(8,128)(2,1)S(1)} %collective-permute-done.12, bf16[336,576]{0,1:T(8,128)(2,1)S(1)} %bitcast.265), kind=kOutput, calls=%fused_computation.31 | convolution fusion | flops 2688270336 | bytes 9400320 | tf_op jit(solution)/shard_map/dot_general | solution.py:31
  368.2 6.8 %reshape.303 = bf16[2,2,2,2,36,3456]{5,4,3,2,1,0:T(8,128)(2,1)} reshape(bf16[576,3456]{1,0:T(8,128)(2,1)} %convolution_convert_fusion.3) | data formatting | bytes 7962624 | tf_op jit(solution)/shard_map/reshape | solution.py:156
  381.1 9.0 %collective-permute-done.9 = bf16[2,2,72,1152]{3,2,0,1:T(8,128)(2,1)} collective-permute-done((bf16[2,2,72,1152]{3,2,0,1:T(8,128)(2,1)S(1)}, bf16[2,2,72,1152]{3,2,0,1:T(8,128)(2,1)}, u32[]{:S(2)}, u32[]{:S(2)}) %collective-permute-start.9) | collective-permute-done | bytes 663584 | tf_op jit(solution)/shard_map/ppermute | solution.py:40
  392.9 9.6 %convolution_convert_fusion.1 = bf16[576,4608]{1,0:T(8,128)(2,1)} fusion(bf16[336,4608]{1,0:T(8,128)(2,1)} %collective-permute-done.25, bf16[336,4608]{1,0:T(8,128)(2,1)} %get-tuple-element.25, bf16[336,576]{0,1:T(8,128)(2,1)} %collective-permute-done.24, bf16[336,576]{0,1:T(8,128)(2,1)S(1)} %bitcast.267), kind=kOutput, calls=%fused_computation.7 | convolution fusion | flops 3583844352 | bytes 12275712 | tf_op jit(solution)/shard_map/dot_general | solution.py:31
  402.5 19.7 %collective-permute-done.10 = bf16[2,72,1152]{2,1,0:T(8,128)(2,1)S(1)} collective-permute-done((bf16[2,72,1152]{2,1,0:T(8,128)(2,1)S(1)}, bf16[2,72,1152]{2,1,0:T(8,128)(2,1)S(1)}, u32[]{:S(2)}, u32[]{:S(2)}) %collective-permute-start.10) | collective-permute-done | bytes 331808 | tf_op jit(solution)/shard_map/ppermute | solution.py:35
  422.3 7.8 %reshape.310 = bf16[2,2,2,2,36,4608]{5,4,3,2,1,0:T(8,128)(2,1)} reshape(bf16[576,4608]{1,0:T(8,128)(2,1)} %convolution_convert_fusion.1) | data formatting | bytes 10616832 | tf_op jit(solution)/shard_map/reshape | solution.py:156
  447.4 17.5 %collective-permute-done.15 = bf16[2,2,36,3456]{3,1,2,0:T(2,128)(2,1)S(1)} collective-permute-done((bf16[2,2,36,3456]{3,1,2,0:T(2,128)(2,1)S(1)}, bf16[2,2,36,3456]{3,1,2,0:T(2,128)(2,1)S(1)}, u32[]{:S(2)}, u32[]{:S(2)}) %collective-permute-start.15) | collective-permute-done | bytes 995360 | tf_op jit(solution)/shard_map/ppermute | solution.py:40
  467.5 8.8 %collective-permute-done.33 = bf16[2,2,144,1152]{3,2,0,1:T(8,128)(2,1)S(1)} collective-permute-done((bf16[2,2,144,1152]{3,2,0,1:T(8,128)(2,1)S(1)}, bf16[2,2,144,1152]{3,2,0,1:T(8,128)(2,1)S(1)}, u32[]{:S(2)}, u32[]{:S(2)}) %collective-permute-start.33) | collective-permute-done | bytes 1327136 | tf_op jit(solution)/shard_map/ppermute | solution.py:40
  476.6 18.3 %collective-permute-done.26 = bf16[2,2,2,36,4608]{4,2,3,1,0:T(2,128)(2,1)S(1)} collective-permute-done((bf16[2,2,2,36,4608]{4,2,3,1,0:T(2,128)(2,1)S(1)}, bf16[2,2,2,36,4608]{4,2,3,1,0:T(2,128)(2,1)S(1)}, u32[]{:S(2)}, u32[]{:S(2)}) %collective-permute-start.26) | collective-permute-done | bytes 2654240 | tf_op jit(solution)/shard_map/ppermute | solution.py:35
  505.4 21.2 %collective-permute-done.27 = bf16[2,2,36,4608]{3,1,2,0:T(2,128)(2,1)S(1)} collective-permute-done((bf16[2,2,36,4608]{3,1,2,0:T(2,128)(2,1)S(1)}, bf16[2,2,36,4608]{3,1,2,0:T(2,128)(2,1)S(1)}, u32[]{:S(2)}, u32[]{:S(2)}) %collective-permute-start.27) | collective-permute-done | bytes 1327136 | tf_op jit(solution)/shard_map/ppermute | solution.py:40
  531.1 19.4 %collective-permute-done.28 = bf16[2,36,4608]{2,0,1:T(2,128)(2,1)S(1)} collective-permute-done((bf16[2,36,4608]{2,0,1:T(2,128)(2,1)S(1)}, bf16[2,36,4608]{2,0,1:T(2,128)(2,1)S(1)}, u32[]{:S(2)}, u32[]{:S(2)}) %collective-permute-start.28) | collective-permute-done | bytes 663584 | tf_op jit(solution)/shard_map/ppermute | solution.py:40
  552.0 15.7 %collective-permute-done.29 = bf16[36,4608]{1,0:T(8,128)(2,1)S(1)} collective-permute-done((bf16[36,4608]{1,0:T(8,128)(2,1)S(1)}, bf16[36,4608]{1,0:T(8,128)(2,1)S(1)}, u32[]{:S(2)}, u32[]{:S(2)}) %collective-permute-start.29) | collective-permute-done | bytes 331808 | tf_op jit(solution)/shard_map/ppermute | solution.py:40
  (334 shorter events, 245.5 us)
Async XLA Ops:
  7.7 17.4 %collective-permute-start.1 = (bf16[336,576]{1,0:T(8,128)(2,1)}, bf16[336,576]{1,0:T(8,128)(2,1)}, u32[]{:S(2)}, u32[]{:S(2)}) collective-permute-start(bf16[336,576]{1,0:T(8,128)(2,1)} %get-tuple-element.50), channel_id=1, source_target_pairs={{0,1},{1,0},{2,3},{3,2},{4,5},{5,4},{6,7},{7,6},{8,9},{9,8},{10,11... | collective-permute-start | bytes 1161224 | tf_op jit(solution)/shard_map/ppermute | solution.py:35
  8.7 47.0 %collective-permute-start.3 = (bf16[168,1152]{1,0:T(8,128)(2,1)}, bf16[168,1152]{1,0:T(8,128)(2,1)}, u32[]{:S(2)}, u32[]{:S(2)}) collective-permute-start(bf16[168,1152]{1,0:T(8,128)(2,1)} %get-tuple-element.53), channel_id=1, source_target_pairs={{0,1},{1,0},{2,3},{3,2},{4,5},{5,4},{6,7},{7,6},{8,9},{9,8},{10,11... | collective-permute-start | bytes 1161224 | tf_op jit(solution)/shard_map/ppermute | solution.py:35
  58.8 259.4 %collective-permute-start.31 = (bf16[336,1152]{1,0:T(8,128)(2,1)}, bf16[336,1152]{1,0:T(8,128)(2,1)}, u32[]{:S(2)}, u32[]{:S(2)}) collective-permute-start(bf16[336,1152]{1,0:T(8,128)(2,1)} %get-tuple-element.23), channel_id=1, source_target_pairs={{0,2},{2,0},{4,6},{6,4},{8,10},{10,8},{12,14},{14,12},{16,18},{18,... | collective-permute-start | bytes 2322440 | tf_op jit(solution)/shard_map/ppermute | solution.py:40
  102.8 174.4 %collective-permute-start.19 = (bf16[336,1152]{1,0:T(8,128)(2,1)}, bf16[336,1152]{1,0:T(8,128)(2,1)}, u32[]{:S(2)}, u32[]{:S(2)}) collective-permute-start(bf16[336,1152]{1,0:T(8,128)(2,1)} %get-tuple-element.28), channel_id=1, source_target_pairs={{0,2},{2,0},{4,6},{6,4},{8,10},{10,8},{12,14},{14,12},{16,18},{18,... | collective-permute-start | bytes 2322440 | tf_op jit(solution)/shard_map/ppermute | solution.py:40
  141.4 154.2 %collective-permute-start.7 = (bf16[336,1152]{1,0:T(8,128)(2,1)}, bf16[336,1152]{1,0:T(8,128)(2,1)}, u32[]{:S(2)}, u32[]{:S(2)}) collective-permute-start(bf16[336,1152]{1,0:T(8,128)(2,1)} %get-tuple-element.30), channel_id=1, source_target_pairs={{0,2},{2,0},{4,6},{6,4},{8,10},{10,8},{12,14},{14,12},{16,18},{18,... | collective-permute-start | bytes 2322440 | tf_op jit(solution)/shard_map/ppermute | solution.py:40
  164.1 147.7 %collective-permute-start.30 = (bf16[336,2304]{1,0:T(8,128)(2,1)}, bf16[336,2304]{1,0:T(8,128)(2,1)}, u32[]{:S(2)}, u32[]{:S(2)}) collective-permute-start(bf16[336,2304]{1,0:T(8,128)(2,1)} %copy.147), channel_id=1, source_target_pairs={{0,2},{2,0},{4,6},{6,4},{8,10},{10,8},{12,14},{14,12},{16,18},{18,... | collective-permute-start | bytes 4644872 | tf_op jit(solution)/shard_map/ppermute | solution.py:40
  276.7 17.2 %collective-permute-start.6 = (bf16[336,1152]{1,0:T(8,128)(2,1)}, bf16[336,1152]{1,0:T(8,128)(2,1)}, u32[]{:S(2)}, u32[]{:S(2)}) collective-permute-start(bf16[336,1152]{1,0:T(8,128)(2,1)} %copy.124), channel_id=1, source_target_pairs={{0,2},{2,0},{4,6},{6,4},{8,10},{10,8},{12,14},{14,12},{16,18},{18,... | collective-permute-start | bytes 2322440 | tf_op jit(solution)/shard_map/ppermute | solution.py:40
  293.9 99.0 %collective-permute-start.25 = (bf16[336,4608]{1,0:T(8,128)(2,1)}, bf16[336,4608]{1,0:T(8,128)(2,1)}, u32[]{:S(2)}, u32[]{:S(2)}) collective-permute-start(bf16[336,4608]{1,0:T(8,128)(2,1)} %get-tuple-element.25), channel_id=1, source_target_pairs={{0,2},{2,0},{4,6},{6,4},{8,10},{10,8},{12,14},{14,12},{16,18},{18,... | collective-permute-start | bytes 9289736 | tf_op jit(solution)/shard_map/ppermute | solution.py:40
  295.6 97.2 %collective-permute-start.24 = (bf16[336,576]{0,1:T(8,128)(2,1)}, bf16[336,576]{0,1:T(8,128)(2,1)}, u32[]{:S(2)}, u32[]{:S(2)}) collective-permute-start(bf16[336,576]{0,1:T(8,128)(2,1)} %bitcast.268), channel_id=1, source_target_pairs={{0,2},{2,0},{4,6},{6,4},{8,10},{10,8},{12,14},{14,12},{16,18},{18,... | collective-permute-start | bytes 1161224 | tf_op jit(solution)/shard_map/ppermute | solution.py:40
  311.7 48.8 %collective-permute-start.13 = (bf16[336,3456]{1,0:T(8,128)(2,1)}, bf16[336,3456]{1,0:T(8,128)(2,1)}, u32[]{:S(2)}, u32[]{:S(2)}) collective-permute-start(bf16[336,3456]{1,0:T(8,128)(2,1)} %copy.130), channel_id=1, source_target_pairs={{0,2},{2,0},{4,6},{6,4},{8,10},{10,8},{12,14},{14,12},{16,18},{18,... | collective-permute-start | bytes 6967304 | tf_op jit(solution)/shard_map/ppermute | solution.py:40
  316.6 38.4 %collective-permute-start.8 = (bf16[2,2,2,72,1152]{4,3,1,2,0:T(8,128)(2,1)}, bf16[2,2,2,72,1152]{4,3,1,2,0:T(8,128)(2,1)S(1)}, u32[]{:S(2)}, u32[]{:S(2)}) collective-permute-start(bf16[2,2,2,72,1152]{4,3,1,2,0:T(8,128)(2,1)} %bitcast.221), channel_id=1, source_target_pairs={{0,8},{2,10},{4,12},{6,14},{8,0},{10,2},{12,4},{14,6},{16,24},{18,... | collective-permute-start | bytes 3981320 | tf_op jit(solution)/shard_map/ppermute | solution.py:40
  318.2 31.3 %collective-permute-start.22 = (bf16[2,36,1152]{2,1,0:T(8,128)(2,1)S(1)}, bf16[2,36,1152]{2,1,0:T(8,128)(2,1)S(1)}, u32[]{:S(2)}, u32[]{:S(2)}) collective-permute-start(bf16[2,36,1152]{2,1,0:T(8,128)(2,1)S(1)} %dynamic-slice_bitcast_fusion.12), channel_id=1, source_target_pairs={{0,16},{2,18},{4,20},{6,22},{8,24},{10,26},{12,28},{14,30},{16,0},... | collective-permute-start | bytes 497672 | tf_op jit(solution)/shard_map/ppermute | solution.py:40
  354.9 88.6 %collective-permute-start.32 = (bf16[2,2,2,144,1152]{4,3,0,1,2:T(8,128)(2,1)}, bf16[2,2,2,144,1152]{4,3,0,1,2:T(8,128)(2,1)}, u32[]{:S(2)}, u32[]{:S(2)}) collective-permute-start(bf16[2,2,2,144,1152]{4,3,0,1,2:T(8,128)(2,1)} %bitcast.217), channel_id=1, source_target_pairs={{0,1},{1,0},{2,3},{3,2},{4,5},{5,4},{6,7},{7,6},{8,9},{9,8},{10,11... | collective-permute-start | bytes 7962632 | tf_op jit(solution)/shard_map/ppermute | solution.py:35
  357.1 33.1 %collective-permute-start.9 = (bf16[2,2,72,1152]{3,2,0,1:T(8,128)(2,1)S(1)}, bf16[2,2,72,1152]{3,2,0,1:T(8,128)(2,1)}, u32[]{:S(2)}, u32[]{:S(2)}) collective-permute-start(bf16[2,2,72,1152]{3,2,0,1:T(8,128)(2,1)S(1)} %dynamic-slice_bitcast_fusion.2), channel_id=1, source_target_pairs={{0,16},{2,18},{4,20},{6,22},{8,24},{10,26},{12,28},{14,30},{16,0},... | collective-permute-start | bytes 1990664 | tf_op jit(solution)/shard_map/ppermute | solution.py:40
  379.7 57.6 %collective-permute-start.14 = (bf16[2,2,2,36,3456]{4,2,3,1,0:T(2,128)(2,1)}, bf16[2,2,2,36,3456]{4,2,3,1,0:T(2,128)(2,1)}, u32[]{:S(2)}, u32[]{:S(2)}) collective-permute-start(bf16[2,2,2,36,3456]{4,2,3,1,0:T(2,128)(2,1)} %bitcast.219), channel_id=1, source_target_pairs={{0,4},{2,6},{4,0},{6,2},{8,12},{10,14},{12,8},{14,10},{16,20},{18,... | collective-permute-start | bytes 5971976 | tf_op jit(solution)/shard_map/ppermute | solution.py:40
  391.5 30.7 %collective-permute-start.10 = (bf16[2,72,1152]{2,1,0:T(8,128)(2,1)S(1)}, bf16[2,72,1152]{2,1,0:T(8,128)(2,1)S(1)}, u32[]{:S(2)}, u32[]{:S(2)}) collective-permute-start(bf16[2,72,1152]{2,1,0:T(8,128)(2,1)S(1)} %dynamic-slice_bitcast_fusion.10), channel_id=1, source_target_pairs={{0,1},{1,0},{2,3},{3,2},{4,5},{5,4},{6,7},{7,6},{8,9},{9,8},{10,11... | collective-permute-start | bytes 995336 | tf_op jit(solution)/shard_map/ppermute | solution.py:35
  435.7 59.1 %collective-permute-start.26 = (bf16[2,2,2,36,4608]{4,2,3,1,0:T(2,128)(2,1)S(1)}, bf16[2,2,2,36,4608]{4,2,3,1,0:T(2,128)(2,1)S(1)}, u32[]{:S(2)}, u32[]{:S(2)}) collective-permute-start(bf16[2,2,2,36,4608]{4,2,3,1,0:T(2,128)(2,1)S(1)} %bitcast.252), channel_id=1, source_target_pairs={{0,1},{1,0},{2,3},{3,2},{4,5},{5,4},{6,7},{7,6},{8,9},{9,8},{10,11... | collective-permute-start | bytes 7962632 | tf_op jit(solution)/shard_map/ppermute | solution.py:35
  440.1 24.8 %collective-permute-start.15 = (bf16[2,2,36,3456]{3,1,2,0:T(2,128)(2,1)S(1)}, bf16[2,2,36,3456]{3,1,2,0:T(2,128)(2,1)S(1)}, u32[]{:S(2)}, u32[]{:S(2)}) collective-permute-start(bf16[2,2,36,3456]{3,1,2,0:T(2,128)(2,1)S(1)} %bitcast.257), channel_id=1, source_target_pairs={{0,8},{2,10},{4,12},{6,14},{8,0},{10,2},{12,4},{14,6},{16,24},{18,... | collective-permute-start | bytes 2985992 | tf_op jit(solution)/shard_map/ppermute | solution.py:40
  446.2 30.1 %collective-permute-start.33 = (bf16[2,2,144,1152]{3,2,0,1:T(8,128)(2,1)S(1)}, bf16[2,2,144,1152]{3,2,0,1:T(8,128)(2,1)S(1)}, u32[]{:S(2)}, u32[]{:S(2)}) collective-permute-start(bf16[2,2,144,1152]{3,2,0,1:T(8,128)(2,1)S(1)} %dynamic-slice_bitcast_fusion), channel_id=1, source_target_pairs={{0,4},{2,6},{4,0},{6,2},{8,12},{10,14},{12,8},{14,10},{16,20},{18,... | collective-permute-start | bytes 3981320 | tf_op jit(solution)/shard_map/ppermute | solution.py:40
  465.6 32.0 %collective-permute-start.16 = (bf16[2,36,3456]{2,0,1:T(2,128)(2,1)S(1)}, bf16[2,36,3456]{2,0,1:T(2,128)(2,1)S(1)}, u32[]{:S(2)}, u32[]{:S(2)}) collective-permute-start(bf16[2,36,3456]{2,0,1:T(2,128)(2,1)S(1)} %bitcast.264), channel_id=1, source_target_pairs={{0,16},{2,18},{4,20},{6,22},{8,24},{10,26},{12,28},{14,30},{16,0},... | collective-permute-start | bytes 1493000 | tf_op jit(solution)/shard_map/ppermute | solution.py:40
  496.7 29.8 %collective-permute-start.27 = (bf16[2,2,36,4608]{3,1,2,0:T(2,128)(2,1)S(1)}, bf16[2,2,36,4608]{3,1,2,0:T(2,128)(2,1)S(1)}, u32[]{:S(2)}, u32[]{:S(2)}) collective-permute-start(bf16[2,2,36,4608]{3,1,2,0:T(2,128)(2,1)S(1)} %bitcast.256), channel_id=1, source_target_pairs={{0,4},{2,6},{4,0},{6,2},{8,12},{10,14},{12,8},{14,10},{16,20},{18,... | collective-permute-start | bytes 3981320 | tf_op jit(solution)/shard_map/ppermute | solution.py:40
  498.6 32.1 %collective-permute-start.34 = (bf16[2,144,1152]{2,1,0:T(8,128)(2,1)S(1)}, bf16[2,144,1152]{2,1,0:T(8,128)(2,1)S(1)}, u32[]{:S(2)}, u32[]{:S(2)}) collective-permute-start(bf16[2,144,1152]{2,1,0:T(8,128)(2,1)S(1)} %dynamic-slice_bitcast_fusion.1), channel_id=1, source_target_pairs={{0,8},{2,10},{4,12},{6,14},{8,0},{10,2},{12,4},{14,6},{16,24},{18,... | collective-permute-start | bytes 1990664 | tf_op jit(solution)/shard_map/ppermute | solution.py:40
  527.4 23.2 %collective-permute-start.28 = (bf16[2,36,4608]{2,0,1:T(2,128)(2,1)S(1)}, bf16[2,36,4608]{2,0,1:T(2,128)(2,1)S(1)}, u32[]{:S(2)}, u32[]{:S(2)}) collective-permute-start(bf16[2,36,4608]{2,0,1:T(2,128)(2,1)S(1)} %bitcast.263), channel_id=1, source_target_pairs={{0,8},{2,10},{4,12},{6,14},{8,0},{10,2},{12,4},{14,6},{16,24},{18,... | collective-permute-start | bytes 1990664 | tf_op jit(solution)/shard_map/ppermute | solution.py:40
  530.9 20.2 %collective-permute-start.35 = (bf16[144,1152]{1,0:T(8,128)(2,1)S(1)}, bf16[144,1152]{1,0:T(8,128)(2,1)S(1)}, u32[]{:S(2)}, u32[]{:S(2)}) collective-permute-start(bf16[144,1152]{1,0:T(8,128)(2,1)S(1)} %dynamic-slice_bitcast_fusion.9), channel_id=1, source_target_pairs={{0,16},{2,18},{4,20},{6,22},{8,24},{10,26},{12,28},{14,30},{16,0},... | collective-permute-start | bytes 995336 | tf_op jit(solution)/shard_map/ppermute | solution.py:40
  (78 other events, 826.9 us)

commit v2 on v1

--- a/solution.py
+++ b/solution.py
@@ -1,6 +1,11 @@
+import functools
+
 import jax
 import jax.numpy as jnp
+import numpy as np
 from jax import lax
+from jax.experimental import pallas as pl
+from jax.experimental.pallas import tpu as pltpu
 from jax.sharding import PartitionSpec as P
 
 HEADS = 16
@@ -48,6 +53,406 @@
     return jnp.where(
         first, jnp.concatenate([own, got], axis=axis), jnp.concatenate([got, own], axis=axis)
     )
+
+
+MESH = pl.DeviceIdType.MESH
+LANES = 384
+TWO = 2 * LANES
+
+
+class Matrix:
+    def __init__(self, share, columns, pieces, cuts):
+        self.share, self.columns = share, columns
+        self.main = share - share % 16
+        self.rest = share % 16
+        self.pieces, start = [], 0
+        for width in pieces:
+            self.pieces.append((start, width))
+            start += width
+        self.cuts = cuts
+        self.fold = self.rest and 16
+        self.fold_width = max(pieces)
+
+    def left_rows(self, blocks):
+        folds = len(self.pieces) if self.rest else 0
+        return blocks * (self.main + folds * 16)
+
+
+class Unit:
+    def __init__(self, matrix, rows, start, columns, hops, folded):
+        self.matrix, self.rows, self.start, self.columns = matrix, rows, start, columns
+        self.hops, self.folded = hops, folded
+
+
+def make_units(matrices, hops_of):
+    units = []
+    for m, matrix in enumerate(matrices):
+        for start, columns in matrix.cuts:
+            units.append(Unit(m, matrix.main, start, columns, hops_of[len(units)], False))
+        if matrix.rest:
+            units.append(Unit(m, 16, 0, matrix.fold_width, hops_of[len(units)], True))
+    return units
+
+
+def reduce_kernel(matrices, units, events, dims, *refs):
+    count = len(matrices)
+    lefts = [(refs[2 * i], refs[2 * i + 1]) for i in range(count)]
+    refs = refs[2 * count :]
+    rights = [(refs[2 * i], refs[2 * i + 1]) for i in range(count)]
+    refs = refs[2 * count :]
+    vector_ref, refs = refs[0], refs[1:]
+    outs, refs = refs[: len(units)], refs[len(units) :]
+    vector_out, refs = refs[0], refs[1:]
+    grads, refs = refs[: len(units)], refs[len(units) :]
+    hops = len(dims)
+    landed = [refs[i * hops : (i + 1) * hops] for i in range(len(units))]
+    refs = refs[len(units) * hops :]
+    vector_land, refs = refs[: hops + 1], refs[hops + 1 :]
+    vector_sum, refs = refs[0], refs[1:]
+    fold_sum, left_buffer, right_buffer, refs = refs[0], refs[1], refs[2], refs[3:]
+    send_sem, recv_sem, vsend_sem, vrecv_sem, left_sem, right_sem = refs
+
+    dp = lax.axis_index("dp")
+    seq = lax.axis_index("seq")
+    core = lax.rem(dp, 2)
+
+    def bit(name):
+        return seq if name == "seq" else lax.rem(lax.div(dp, 1 << name), 2)
+
+    def partner(name):
+        if name == "seq":
+            return (dp, 1 - seq)
+        return (dp + (1 - 2 * bit(name)) * (1 << name), seq)
+
+    barrier = pltpu.get_barrier_semaphore()
+    for name in [0] + list(dims):
+        pl.semaphore_signal(barrier, inc=1, device_id=partner(name), device_id_type=MESH)
+    pl.semaphore_wait(barrier, len(dims) + 1)
+
+    def left_copies(m):
+        rows = matrices[m].left_rows(2 ** len(dims))
+        return [
+            pltpu.make_async_copy(
+                lefts[m][k],
+                left_buffer.at[m % 2, pl.ds(0, rows), pl.ds(k * LANES, LANES)],
+                left_sem.at[m % 2, k],
+            )
+            for k in range(2)
+        ]
+
+    all_pieces = [(m, p) for m, matrix in enumerate(matrices) for p in range(len(matrix.pieces))]
+
+    def right_copies(index):
+        m, p = all_pieces[index]
+        start, width = matrices[m].pieces[p]
+        return [
+            pltpu.make_async_copy(
+                rights[m][k].at[:, pl.ds(start, width)],
+                right_buffer.at[index % 2, pl.ds(k * LANES, LANES), pl.ds(0, width)],
+                right_sem.at[index % 2, k],
+            )
+            for k in range(2)
+        ]
+
+    def start(copies):
+        for copy in copies:
+            copy.start()
+
+    def wait(copies):
+        for copy in copies:
+            copy.wait()
+
+    for m in range(2):
+        start(left_copies(m))
+    for index in range(2):
+        start(right_copies(index))
+
+    sent = []
+
+    def send(u, h):
+        unit = units[u]
+        index = []
+        for name in dims:
+            if name in unit.hops[:h]:
+                index.append(bit(name))
+            elif name == unit.hops[h]:
+                index.append(1 - bit(name))
+            else:
+                index.append(slice(None))
+        copy = pltpu.make_async_remote_copy(
+            src_ref=grads[u].at[tuple(index)],
+            dst_ref=landed[u][h],
+            send_sem=send_sem.at[u, h],
+            recv_sem=recv_sem.at[u, h],
+            device_id=partner(unit.hops[h]),
+            device_id_type=MESH,
+        )
+        copy.start()
+        sent.append(copy)
+        return copy
+
+    flying = {}
+
+    def add(u, h):
+        unit = units[u]
+        flying[u, h].wait_recv()
+        done = unit.hops[: h + 1]
+        free = [name for name in dims if name not in done]
+        step = 16
+        last = h + 1 == hops
+
+        @pl.loop(0, 2 ** len(free) * (unit.rows // step))
+        def _(i):
+            block, row = lax.div(i, unit.rows // step), lax.rem(i, unit.rows // step) * step
+            place = {
+                name: lax.rem(lax.div(block, 1 << (len(free) - 1 - k)), 2)
+                for k, name in enumerate(free)
+            }
+            rows = pl.ds(pl.multiple_of(row, step), step)
+            own = tuple(place.get(name, bit(name)) for name in dims) + (rows,)
+            got = tuple(place[name] for name in free) + (rows,)
+            total = grads[u][own].astype(jnp.float32) + landed[u][h][got].astype(jnp.float32)
+            if last:
+                outs[u][rows] = total
+            else:
+                grads[u][own] = total.astype(jnp.bfloat16)
+
+        if not last:
+            flying[u, h + 1] = send(u, h + 1)
+
+    def multiply(index):
+        m, p = all_pieces[index]
+        matrix = matrices[m]
+        start_column, width = matrix.pieces[p]
+        blocks = 2 ** len(dims)
+        if p == 0:
+            wait(left_copies(m))
+        wait(right_copies(index))
+        left, right = left_buffer.at[m % 2], right_buffer.at[index % 2]
+        u = next(
+            i
+            for i, unit in enumerate(units)
+            if unit.matrix == m
+            and not unit.folded
+            and unit.start <= start_column < unit.start + unit.columns
+        )
+        group = blocks
+        while group * matrix.main > 640:
+            group //= 2
+        free = group.bit_length() - 1
+        step = next(s for s in (384, 640, 512, 128) if width % s == 0)
+
+        @pl.loop(0, (blocks // group) * (width // step))
+        def _(i):
+            g, j = lax.div(i, width // step), lax.rem(i, width // step)
+            rows = pl.ds(pl.multiple_of(g * (group * matrix.main), 16), group * matrix.main)
+            columns = pl.ds(pl.multiple_of(j * step, 128), step)
+            result = jnp.dot(left[rows, :], right[:, columns], preferred_element_type=jnp.float32)
+            high = len(dims) - free
+            where = tuple(lax.rem(lax.div(g, 1 << (high - 1 - k)), 2) for k in range(high))
+            target = pl.ds(pl.multiple_of(start_column - units[u].start + j * step, 128), step)
+            grads[u][where + (slice(None),) * (free + 1) + (target,)] = result.astype(
+                jnp.bfloat16
+            ).reshape((2,) * free + (matrix.main, step))
+
+        if matrix.rest:
+            offset = blocks * (matrix.main + 16 * p)
+
+            @pl.loop(0, width // step)
+            def _(j):
+                columns = pl.ds(pl.multiple_of(j * step, 128), step)
+                result = jnp.dot(
+                    left[pl.ds(offset, blocks * 16), :],
+                    right[:, columns],
+                    preferred_element_type=jnp.float32,
+                )
+                if p == 0:
+                    fold_sum[:, columns] = result
+                else:
+                    fold_sum[:, columns] += result
+
+        if index + 2 < len(all_pieces):
+            start(right_copies(index + 2))
+        last = p + 1 == len(matrix.pieces)
+        if last and m + 2 < count:
+            start(left_copies(m + 2))
+        if start_column + width == units[u].start + units[u].columns:
+            flying[u, 0] = send(u, 0)
+        if last and matrix.rest:
+            f = next(i for i, unit in enumerate(units) if unit.matrix == m and unit.folded)
+            folded = fold_sum[:, pl.ds(0, units[f].columns)].astype(jnp.bfloat16)
+            grads[f][...] = folded.reshape((2,) * len(dims) + (16, units[f].columns))
+            flying[f, 0] = send(f, 0)
+
+    def vector_send(h):
+        name = 0 if h == 0 else dims[h - 1]
+        source = vector_ref.at[1 - core] if h == 0 else vector_sum.at[
+            tuple(bit(n) for n in dims[: h - 1]) + (1 - bit(name),)
+        ]
+        copy = pltpu.make_async_remote_copy(
+            src_ref=source,
+            dst_ref=vector_land[h],
+            send_sem=vsend_sem.at[h],
+            recv_sem=vrecv_sem.at[h],
+            device_id=partner(name),
+            device_id_type=MESH,
+        )
+        copy.start()
+        sent.append(copy)
+        return copy
+
+    vector_flying = {}
+
+    def vector_add(h):
+        vector_flying[h].wait_recv()
+        own = tuple(bit(n) for n in dims[:h])
+        if h == 0:
+            vector_sum[...] = vector_ref[core] + vector_land[0][...]
+        elif h < hops:
+            vector_sum[own] = vector_sum[own] + vector_land[h][...]
+        else:
+            vector_out[...] = vector_sum[own] + vector_land[h][...]
+        if h < hops:
+            vector_flying[h + 1] = vector_send(h + 1)
+
+    vector_flying[0] = vector_send(0)
+    vector_done, since = 0, 0
+    for event in events:
+        if event[0] == "c":
+            multiply(event[1])
+        else:
+            add(*event)
+            since += 1
+            if since % 4 == 0 and vector_done <= hops:
+                vector_add(vector_done)
+                vector_done += 1
+    while vector_done <= hops:
+        vector_add(vector_done)
+        vector_done += 1
+    for copy in sent:
+        copy.wait_send()
+
+
+def left_operand(values, matrix, blocks, core_count):
+    rows, depth = values.shape
+    padded = jnp.pad(values, ((0, LANES - rows), (0, 0)))
+    if not matrix.rest:
+        parts = padded.T.reshape(blocks // 2, core_count, 2, matrix.share, LANES)
+        return parts.transpose(1, 0, 2, 3, 4).reshape(core_count, -1, LANES)
+    folds = len(matrix.pieces)
+    size = matrix.left_rows(blocks)
+    row = np.arange(core_count * size)
+    at_core, at = row // size, row % size
+    body = at < blocks * matrix.main
+    fold_at = np.maximum(at - blocks * matrix.main, 0)
+    piece, fold_row = fold_at // (blocks * 16), fold_at % (blocks * 16)
+    block = np.where(body, at // max(matrix.main, 1), fold_row // 16)
+    inner = np.where(body, at % max(matrix.main, 1), matrix.main + fold_row % 16 - piece * matrix.rest)
+    inside = body | ((fold_row % 16 >= piece * matrix.rest) & (fold_row % 16 < (piece + 1) * matrix.rest))
+    column = ((block // 2 * core_count + at_core) * 2 + block % 2) * matrix.share + inner
+    column = jnp.asarray(np.where(inside, column, -1), jnp.int32)
+    choose = (column[:, None] == jnp.arange(depth, dtype=jnp.int32)[None, :]).astype(jnp.bfloat16)
+    picked = lax.dot_general(
+        choose, padded, (((1,), (1,)), ((), ())), preferred_element_type=jnp.float32
+    )
+    return picked.astype(jnp.bfloat16).reshape(core_count, size, LANES)
+
+
+HOPS = {
+    "xyz": ("seq", 1, 2, 3),
+    "yxz": (1, "seq", 2, 3),
+    "yzx": (1, 2, 3, "seq"),
+    "zxy": (2, 3, "seq", 1),
+    "zyx": (2, 3, 1, "seq"),
+    "xzy": ("seq", 2, 3, 1),
+}
+HOP_PLAN = ["xyz", "zxy", "yzx", "yzx", "xyz", "xyz", "zyx", "yxz", "xyz", "yxz", "xyz", "xyz", "xyz", "xyz", "yzx", "xyz", "xzy"]
+EVENTS = [
+    ("c", 0), ("c", 1), ("c", 2), ("c", 3), ("c", 4), ("c", 5), ("c", 6), ("c", 7), ("c", 8),
+    ("c", 9), ("c", 10), (0, 0), (1, 0), ("c", 11), (2, 0), ("c", 12), ("c", 13), (4, 0),
+    ("c", 14), (6, 0), (3, 0), (5, 0), (7, 0), (9, 0), (1, 1), (2, 1), (0, 1), (8, 0), (6, 1),
+    (3, 1), (10, 0), (2, 2), (14, 0), (0, 2), (3, 2), (4, 1), (11, 0), (5, 1), (0, 3), (14, 1),
+    (8, 1), (4, 2), (6, 2), (5, 2), (12, 0), (14, 2), (10, 1), (4, 3), (13, 0), (8, 2), (5, 3),
+    (11, 1), (8, 3), (10, 2), (12, 1), (15, 0), (11, 2), (10, 3), (13, 1), (16, 0), (12, 2),
+    (11, 3), (7, 1), (9, 1), (13, 2), (15, 1), (16, 1), (12, 3), (13, 3), (1, 2), (7, 2), (9, 2),
+    (16, 2), (2, 3), (3, 3), (15, 2), (1, 3), (7, 3), (16, 3), (6, 3), (9, 3), (14, 3), (15, 3),
+]
+
+
+def weight_gradients(pairs, lines, plan, bits):
+    matrices, units, events = plan
+    blocks = 2**bits
+    dims = list(reversed(range(1, bits))) + ["seq"]
+    core = lax.axis_index("dp") & 1
+    operands = []
+    for (left, _), matrix in zip(pairs, matrices):
+        both = left_operand(left, matrix, blocks, 2)
+        operands += [pick(both, core, 0), swap_dp(pick(both, 1 - core, 0), 0)]
+    for _, right in pairs:
+        padded = jnp.pad(right, ((0, LANES - right.shape[0]), (0, 0)))
+        operands += [padded, swap_dp(padded, 0)]
+    operands.append(lines)
+    anywhere = pl.BlockSpec(memory_space=pl.ANY)
+    vmem = pl.BlockSpec(memory_space=pltpu.VMEM)
+    hops = len(dims)
+    outs = [jax.ShapeDtypeStruct((unit.rows, unit.columns), jnp.float32) for unit in units]
+    outs.append(jax.ShapeDtypeStruct(lines.shape[-2:], jnp.float32))
+    low = jnp.bfloat16
+    scratch = [pltpu.VMEM((2,) * hops + (unit.rows, unit.columns), low) for unit in units]
+    for unit in units:
+        for h in range(hops):
+            scratch.append(pltpu.VMEM((2,) * (hops - 1 - h) + (unit.rows, unit.columns), low))
+    tail = lines.shape[-2:]
+    for h in range(hops + 1):
+        scratch.append(pltpu.VMEM((2,) * (hops - h) + tail, jnp.float32))
+    scratch.append(pltpu.VMEM((2,) * hops + tail, jnp.float32))
+    folded = [matrix.fold_width for matrix in matrices if matrix.rest]
+    scratch.append(pltpu.VMEM((blocks * 16, max(folded)), jnp.float32))
+    scratch.append(pltpu.VMEM((2, max(m.left_rows(blocks) for m in matrices), TWO), low))
+    scratch.append(pltpu.VMEM((2, TWO, max(max(w for _, w in m.pieces) for m in matrices)), low))
+    scratch += [pltpu.SemaphoreType.DMA((len(units), hops))] * 2
+    scratch += [pltpu.SemaphoreType.DMA((hops + 1,))] * 2
+    scratch += [pltpu.SemaphoreType.DMA((2, 2))] * 2
+    results = pl.pallas_call(
+        functools.partial(reduce_kernel, matrices, units, events, dims),
+        out_shape=outs,
+        in_specs=[anywhere] * (4 * len(matrices)) + [vmem],
+        out_specs=[vmem] * len(outs),
+        scratch_shapes=scratch,
+        compiler_params=pltpu.CompilerParams(
+            collective_id=0, has_side_effects=True, vmem_limit_bytes=62 * 2**20
+        ),
+        name="reduce_weights",
+    )(*operands)
+    wholes = []
+    for m, matrix in enumerate(matrices):
+        mains = [r for r, u in zip(results, units) if u.matrix == m and not u.folded]
+        whole = jnp.concatenate(mains, axis=1) if len(mains) > 1 else mains[0]
+        if matrix.rest:
+            fold = next(r for r, u in zip(results, units) if u.matrix == m and u.folded)
+            parts = [
+                fold[p * matrix.rest : (p + 1) * matrix.rest, :width]
+                for p, (_, width) in enumerate(matrix.pieces)
+            ]
+            whole = jnp.concatenate([whole, jnp.concatenate(parts, axis=1)], axis=0)
+        wholes.append(whole)
+    return wholes, results[-1]
+
+
+def even_cuts(columns, width):
+    return [(start, width) for start in range(0, columns, width)]
+
+
+def make_plan(width, hidden, chunks):
+    matrices = [
+        Matrix(hidden // chunks, width, [384] * 3, even_cuts(width, 384)),
+        Matrix(width // chunks, hidden, [1152] * 4, even_cuts(hidden, 1152)),
+        Matrix(width // chunks, width, [384] * 3, [(0, width)]),
+        Matrix(width // chunks, 3 * width, [1152] * 3, even_cuts(3 * width, 1152)),
+        Matrix(2 * width // chunks, width, [640, 512], [(0, 640), (640, 512)]),
+    ]
+    units = make_units(matrices, [HOPS[name] for name in HOP_PLAN])
+    return matrices, units, EVENTS
 
 
 def halving(block, order, bits):
@@ -160,18 +565,15 @@
     order_y = above + ["seq"]
     order_z = above[1:] + ["seq"] + above[:1]
 
-    grad_fc2 = halving(own_rows(acted_low, grad_out), order_x, bits)
     grad_fc2_bias = column_sum(grad_out)
     grad_acted = matmul(grad_out, fc2_weight.T)
     grad_hidden = gelu_back(grad_acted)[0].astype(jnp.bfloat16)
-    grad_fc1 = halving(own_rows(normed_two, grad_hidden), order_x, bits)
     grad_fc1_bias = column_sum(grad_hidden)
     grad_normed_two = matmul(grad_hidden, fc1_weight.T)
     _, norm_back_two = jax.vjp(layer_norm, stream_two, gain_two, shift_two)
     back_two, grad_gain_two, grad_shift_two = norm_back_two(grad_normed_two)
     grad_stream_two = grad_out.astype(jnp.float32) + back_two
     grad_attended = grad_stream_two.astype(jnp.bfloat16)
-    grad_proj = halving(own_rows(mixed, grad_attended), order_y, bits)
     grad_proj_bias = column_sum(grad_attended)
     grad_mixed = matmul(grad_attended, proj_weight.T)
     grad_mixed = grad_mixed.astype(jnp.bfloat16).reshape(rows, HEADS, HEAD_DIM)
@@ -183,12 +585,10 @@
     grad_keys = product("hqk,qhd->khd", grad_scores, query) * scale
     grad_packed = jnp.stack([grad_query, grad_keys, grad_values], axis=1)
     grad_packed = grad_packed.astype(jnp.bfloat16).reshape(rows, 3 * width)
-    grad_qkv = halving(own_rows(normed, grad_packed), order_y, bits)
     grad_normed = matmul(grad_packed, qkv_weight.T)
     _, norm_back_one = jax.vjp(layer_norm, stream, gain_one, shift_one)
     back_one, grad_gain_one, grad_shift_one = norm_back_one(grad_normed)
     grad_stream = (grad_stream_two + back_one).astype(jnp.bfloat16)
-    grad_skip = halving(own_rows(joined, grad_stream), order_z, bits)
     grad_skip_bias = column_sum(grad_stream)
     grad_joined = matmul(grad_stream, skip_weight.T)
 
@@ -203,8 +603,27 @@
         grad_fc2_bias,
     )
     chunks = dp_count * seq_count
+    pairs = [
+        (acted_low, grad_out),
+        (normed_two, grad_hidden),
+        (mixed, grad_attended),
+        (normed, grad_packed),
+        (joined, grad_stream),
+    ]
     line = jnp.concatenate([v.reshape(chunks, -1) for v in vectors], axis=1)
-    line = lax.psum_scatter(line, ("dp", "seq"), scatter_dimension=0, tiled=True)[0]
+    used = line.shape[1]
+    if chunks == 32:
+        lines = jnp.pad(line, ((0, 0), (0, 8 * 128 - used)))
+        lines = lines.reshape((2,) * (bits - 1) + (2, 2, 8, 128))
+        lines = jnp.moveaxis(lines, bits - 1, 0)
+        plan = make_plan(width, fc1_weight.shape[1], chunks)
+        weights, line = weight_gradients(pairs, lines, plan, bits)
+        line = line.reshape(-1)
+    else:
+        orders = [order_x, order_x, order_y, order_y, order_z]
+        weights = [halving(own_rows(*p), o, bits) for p, o in zip(pairs, orders)]
+        line = lax.psum_scatter(line, ("dp", "seq"), scatter_dimension=0, tiled=True)[0]
+    grad_fc2, grad_fc1, grad_proj, grad_qkv, grad_skip = weights
     pieces, start = [], 0
     for vector in vectors:
         size = vector.shape[0] // chunks

time: 576 us -> 441 us (0.77)
  Pallas kernels: 0 us -> 187 us
  waiting for transfers between devices: 183 us -> 17 us
  blocking collectives: 41.8 us -> 0 us
  other arithmetic: 70 us -> 36 us
  local copies, waits for them, and re-layouts: 108 us -> 77.5 us
  starting transfers between devices: 41.2 us -> 11.6 us
  matrix products: 123 us -> 105 us
    pallas_call x0 -> x1, Pallas kernels: none -> 187 us  [weight_gradients(): pl.pallas_call(functools.partial(reduce_kernel, matrices, units, events,...]
    ppermute x25 -> x10, waiting for transfers between devices: 122 us -> 3.96 us  [swap_dp(): return lax.ppermute(values, 'dp', [(i, i ^ 1 << bit) for i in range(count)])]
    ppermute x11 -> x6, waiting for transfers between devices: 61.1 us -> 13.1 us  [swap_seq(): return lax.ppermute(values, 'seq', [(0, 1), (1, 0)])]
    unnamed x1 -> x0, blocking collectives: 41.8 us -> none
    dot_general x15 -> x10, matrix products: 106 us -> 66.3 us  [matmul(): return jnp.dot(left, right, preferred_element_type=jnp.float32)]
    dynamic_slice x26 -> x1, local copies, waits for them, and re-layouts: 39.1 us -> 0.58 us  [pick(): return lax.dynamic_index_in_dim(values, index, axis, keepdims=False)]
    ppermute x25 -> x10, starting transfers between devices: 28.6 us -> 2.49 us  [swap_dp(): return lax.ppermute(values, 'dp', [(i, i ^ 1 << bit) for i in range(count)])]
    dot_general x0 -> x4, matrix products: none -> 25 us  [left_operand(): lax.dot_general(choose, padded, (((1,), (1,)), ((), ())), preferred_eleme...]
  transfers between devices with their start and end apart: 36 -> 16, of which waited for: 17 -> 3; matrix products, arithmetic and copies ran while one was open for 51% -> 22% of each run, Pallas kernels for 0% -> 0%
where the time goes in v2:
time: 441 us; the launch traced here: 436 us
  Pallas kernels  187 us (42%)
  matrix products  105 us (24%)
  local copies, waits for them, and re-layouts  77.5 us (18%)
  other arithmetic  36 us (8%)
  waiting for transfers between devices  17 us (4%)
  starting transfers between devices  11.6 us (3%)
    pallas_call x1, Pallas kernels, weight_gradients(): pl.pallas_call(functools.partial(reduce_kernel, matrices, units, events,...  187 us
    dot_general x10, matrix products, matmul(): return jnp.dot(left, right, preferred_element_type=jnp.float32)  66.3 us
    dot_general x4, matrix products, left_operand(): lax.dot_general(choose, padded, (((1,), (1,)), ((), ())), preferred_eleme...  25 us
    unnamed x164, local copies, waits for them, and re-layouts  15.6 us
    dot_general x6, matrix products, product(): return jnp.einsum(spec, left, right, preferred_element_type=jnp.float32)  14.1 us
    squeeze x8, local copies, waits for them, and re-layouts, pick(): return lax.dynamic_index_in_dim(values, index, axis, keepdims=False)  13.5 us
    ppermute x6, waiting for transfers between devices, swap_seq(): return lax.ppermute(values, 'seq', [(0, 1), (1, 0)])  13.1 us
    reshape x8, local copies, waits for them, and re-layouts, local(): line = jnp.concatenate([v.reshape(chunks, -1) for v in vectors], axis=1)  10.6 us
  transfers between devices with their start and end apart: 16, of which 3 were waited for; matrix products, arithmetic and copies ran while one was open for 22% of the time, Pallas kernels for 0%

profile of v2, /device:TPU:0, one launch (start us, length us, event | category | flops | bytes accessed | tf_op | source)
XLA Modules:
  0.0 435.9 jit_solution(16436666049278261187)
XLA Ops:
  10.4 5.3 %collective-permute-done.1 = bf16[336,576]{1,0:T(8,128)(2,1)S(1)} collective-permute-done((bf16[336,576]{1,0:T(8,128)(2,1)S(1)}, bf16[336,576]{1,0:T(8,128)(2,1)S(1)}, u32[]{:S(2)}, u32[]{:S(2)}) %collective-permute-start.1) | collective-permute-done | bytes 387104 | tf_op jit(solution)/shard_map/ppermute | solution.py:40
  16.2 7.8 %collective-permute-done = bf16[168,1152]{1,0:T(8,128)(2,1)S(1)} collective-permute-done((bf16[168,1152]{1,0:T(8,128)(2,1)S(1)}, bf16[168,1152]{1,0:T(8,128)(2,1)S(1)}, u32[]{:S(2)}, u32[]{:S(2)}) %collective-permute-start) | collective-permute-done | bytes 387104 | tf_op jit(solution)/shard_map/ppermute | solution.py:40
  24.3 5.3 %fusion.68 = (f32[336]{0:T(512)S(1)}, f32[336,1152]{1,0:T(8,128)S(1)}) fusion(f32[1152]{0:T(1024)S(1)} %copy-done.57, bf16[2304,1152]{1,0:T(8,128)(2,1)} %param.25, bf16[336,1152]{1,0:T(8,128)(2,1)S(1)} %maximum_select_fusion.3, bf16[336,1152]{1,0:T(8,128)(2,1)S(1)} %maximum_select_fusion.2), kind=kOutput, calls=%fused_computation.159 | convolution fusion | flops 1787498112 | bytes 8410944 | tf_op jit(solution)/shard_map/dot_general | solution.py:36
  32.0 4.8 %convolution_convert_fusion = bf16[336,3456]{1,0:T(8,128)(2,1)} fusion(bf16[336,1152]{1,0:T(8,128)(2,1)S(1)} %add_convert_fusion.3, bf16[1152,3456]{1,0:T(8,128)(2,1)S(1)} %bitcast.147), kind=kOutput, calls=%fused_computation.36 | convolution fusion | flops 2676602880 | bytes 11059200 | tf_op jit(solution)/shard_map/dot_general | solution.py:36
  36.7 4.5 %copy.47 = bf16[336,3456]{0,1:T(8,128)(2,1)S(1)} copy(bf16[336,3456]{1,0:T(8,128)(2,1)} %convolution_convert_fusion) | data formatting | bytes 4644864 | tf_op jit(solution)/shard_map/convert_element_type | solution.py:523
  42.5 3.7 fusion.69
  47.3 3.2 copy-done.11
  53.8 7.7 %convolution_add_fusion = f32[336,4608]{1,0:T(8,128)S(1)} fusion(bf16[336,1152]{1,0:T(8,128)(2,1)S(1)} %add_convert_fusion.2, bf16[1152,4608]{1,0:T(8,128)(2,1)} %param.34, f32[4608]{0:T(1024)S(1)} %copy-done.56), kind=kOutput, calls=%fused_computation.15 | convolution fusion | flops 3568803840 | bytes 17602560 | tf_op jit(solution)/shard_map/dot_general | solution.py:36
  64.2 20.7 %convert_reduce_fusion = (f32[4608]{0:T(1024)}, bf16[336,4608]{1,0:T(8,128)(2,1)S(1)}, f32[336,4608]{1,0:T(8,128)}) fusion(f32[336,4608]{1,0:T(8,128)S(1)} %convolution_add_fusion, bf16[336,1152]{1,0:T(8,128)(2,1)S(1)} %get-tuple-element.59, bf16[4608,1152]{1,0:T(8,128)(2,1)S(1)} %bitcast.145), kind=kOutput, calls=%fused_computation.18 | convolution fusion | flops 3681824256 | bytes 26892288 | tf_op jit(solution)/shard_map/dot_general | solution.py:36
  84.9 10.2 %multiply_reduce_fusion.1 = (f32[1152]{0:T(1024)}, f32[336]{0:T(512)S(1)}, f32[1152]{0:T(1024)}, f32[336,1152]{1,0:T(8,128)S(1)}) fusion(f32[336,1152]{1,0:T(8,128)S(1)} %get-tuple-element.111, f32[336]{0:T(512)S(1)} %fusion.53, f32[336]{0:T(512)S(1)} %broadcast_multiply_fusion, f32[1152]{0:T(1024)S(1)} %copy-done.50, ...), kind=kOutput, calls=%fused_computation.70 | convolution fusion | flops 3570349568 | bytes 16827840 | tf_op jit(solution)/shard_map/dot_general | solution.py:36
  103.1 5.1 %fusion.37 = bf16[336,1,16,72]{0,3,2,1:T(8,128)(2,1)S(1)} fusion(bf16[336,16,72]{0,2,1:T(8,128)(2,1)} %bitcast.138, f32[16,336,336]{1,2,0:T(8,128)} %copy-done.11, f32[16,336]{1,0:T(8,128)S(1)} %get-tuple-element.108), kind=kOutput, calls=%fused_computation.83 | convolution fusion | flops 264112128 | bytes 8795136 | tf_op jit(solution)/shard_map/hqk,qhd->khd/dot_general | solution.py:533
  108.2 4.4 %multiply_reduce_fusion = (f32[16,336]{1,0:T(8,128)S(1)}, f32[16,336,336]{1,2,0:T(8,128)S(1)}) fusion(f32[16,336,336]{1,2,0:T(8,128)} %copy-done.11, f32[16,336]{1,0:T(8,128)S(1)} %get-tuple-element.108, bf16[336,16,72]{0,2,1:T(8,128)(2,1)S(1)} %bitcast.139, bf16[336,3,16,72]{0,3,2,1:T(8,128)(2,1)S(1)} %bitcast.121), kind=kOutput, calls=%fused_computation.11 | convolution fusion | flops 265526016 | bytes 16266240 | tf_op jit(solution)/shard_map/qhd,khd->hqk/dot_general | solution.py:533
  118.5 4.7 %multiply_reduce_fusion.2 = (f32[1152]{0:T(1024)}, f32[336]{0:T(512)S(1)}, f32[1152]{0:T(1024)}, f32[336,1152]{1,0:T(8,128)S(1)}) fusion(f32[336,1152]{1,0:T(8,128)S(1)} %copy-done.6, f32[336]{0:T(512)S(1)} %fusion.52, f32[336]{0:T(512)S(1)} %broadcast_multiply_fusion.1, f32[1152]{0:T(1024)S(1)} %copy-done.51, bf16[336,3456]{0,1:T(8,128)(2,1)S(1)} %bitcast.126, ...), kind=kOutput, calls=%fused_computation.72 | convolution fusion | flops 2678535680 | bytes 13399488 | tf_op jit(solution)/shard_map/dot_general | solution.py:36
  131.0 5.2 %fusion.17 = bf16[2560,384]{1,0:T(8,128)(2,1)} fusion(s32[2560]{0:T(1024)S(1)} %copy-done.65, bf16[336,1152]{0,1:T(8,128)(2,1)S(1)} %bitcast.153), kind=kOutput, calls=%fused_computation.38 | convolution fusion | flops 2268856320 | bytes 2750464 | tf_op jit(solution)/shard_map/dot_general | solution.py:355
  136.2 5.3 %fusion.18 = bf16[2560,384]{1,0:T(8,128)(2,1)} fusion(s32[2560]{0:T(1024)S(1)} %copy-done.65, bf16[336,1152]{1,0:T(8,128)(2,1)S(1)} %copy-done.44), kind=kOutput, calls=%fused_computation.39 | convolution fusion | flops 2268856320 | bytes 2750464 | tf_op jit(solution)/shard_map/dot_general | solution.py:355
  149.7 7.1 %fusion.25 = bf16[336,1152]{1,0:T(8,128)(2,1)S(1)} fusion(f32[336,1152]{1,0:T(8,128)S(1)} %copy-done.3, bf16[336,4608]{1,0:T(8,128)(2,1)S(1)} %multiply_convert_fusion.1, bf16[4608,1152]{1,0:T(8,128)(2,1)} %param.36, f32[1152]{0:T(1024)S(1)} %copy-done.59), kind=kOutput, calls=%fused_computation.52 | convolution fusion | flops 3568416768 | bytes 16040448 | tf_op jit(solution)/shard_map/dot_general | solution.py:36
  159.9 3.7 copy.53
  163.5 4.3 copy.54
  167.8 5.0 %fusion.19 = bf16[3072,384]{1,0:T(8,128)(2,1)S(1)} fusion(s32[3072]{0:T(1024)S(1)} %copy-done.64, bf16[336,1152]{1,0:T(8,128)(2,1)S(1)} %copy-done.42), kind=kOutput, calls=%fused_computation.40 | convolution fusion | flops 2722627584 | bytes 3145728 | tf_op jit(solution)/shard_map/dot_general | solution.py:355
  173.4 9.6 %fusion.16 = bf16[3072,384]{1,0:T(8,128)(2,1)} fusion(s32[3072]{0:T(1024)S(1)} %copy-done.63, bf16[336,2304]{1,0:T(8,128)(2,1)S(1)} %copy-done.29), kind=kOutput, calls=%fused_computation.37 | convolution fusion | flops 5444075520 | bytes 3919872 | tf_op jit(solution)/shard_map/dot_general | solution.py:355
  184.6 4.4 %copy.55 = bf16[336,3456]{1,0:T(8,128)(2,1)} copy(bf16[336,3456]{0,1:T(8,128)(2,1)} %bitcast.127) | data formatting | bytes 4644864 | tf_op jit(solution)/shard_map/convert_element_type | solution.py:587
  193.2 3.4 pad.46.refs_16_
  219.0 3.9 collective-permute-done.15.refs_19_
  234.8 186.5 %reduce_weights.1 = (f32[144,384]{1,0:T(8,128)}, f32[144,384]{1,0:T(8,128)}, f32[144,384]{1,0:T(8,128)}, f32[32,1152]{1,0:T(8,128)}, f32[32,1152]{1,0:T(8,128)},...) custom-call(bf16[2304,384]{1,0:T(8,128)(2,1)} %get-tuple-element.72., ...), custom_call_target="tpu_custom_call" | custom-call | tf_op jit(solution)/shard_map/reduce_weights/pallas_call | solution.py:416
  (276 shorter events, 108.4 us)
Async XLA Ops:
  2.0 22.3 %copy-start.57 = (f32[1152]{0:T(1024)S(1)}, f32[1152]{0:T(1024)}, u32[]{:S(2)}) copy-start(f32[1152]{0:T(1024)} %param.26) | copy-start | bytes 13828
  2.0 13.7 %collective-permute-start.1 = (bf16[336,576]{1,0:T(8,128)(2,1)S(1)}, bf16[336,576]{1,0:T(8,128)(2,1)S(1)}, u32[]{:S(2)}, u32[]{:S(2)}) collective-permute-start(bf16[336,576]{1,0:T(8,128)(2,1)S(1)} %get-tuple-element.82), channel_id=1, source_target_pairs={{0,1},{1,0},{2,3},{3,2},{4,5},{5,4},{6,7},{7,6},{8,9},{9,8},{10,11... | collective-permute-start | bytes 1161224 | tf_op jit(solution)/shard_map/ppermute | solution.py:40
  6.1 17.9 %collective-permute-start = (bf16[168,1152]{1,0:T(8,128)(2,1)S(1)}, bf16[168,1152]{1,0:T(8,128)(2,1)S(1)}, u32[]{:S(2)}, u32[]{:S(2)}) collective-permute-start(bf16[168,1152]{1,0:T(8,128)(2,1)S(1)} %get-tuple-element.88), channel_id=1, source_target_pairs={{0,1},{1,0},{2,3},{3,2},{4,5},{5,4},{6,7},{7,6},{8,9},{9,8},{10,11... | collective-permute-start | bytes 1161224 | tf_op jit(solution)/shard_map/ppermute | solution.py:40
  7.2 54.4 %collective-permute-start.3 = (bf16[168,1152]{1,0:T(8,128)(2,1)}, bf16[168,1152]{1,0:T(8,128)(2,1)}, u32[]{:S(2)}, u32[]{:S(2)}) collective-permute-start(bf16[168,1152]{1,0:T(8,128)(2,1)} %get-tuple-element.85), channel_id=1, source_target_pairs={{0,1},{1,0},{2,3},{3,2},{4,5},{5,4},{6,7},{7,6},{8,9},{9,8},{10,11... | collective-permute-start | bytes 1161224 | tf_op jit(solution)/shard_map/ppermute | solution.py:40
  53.0 42.1 %copy-start.2 = (f32[336,1152]{1,0:T(8,128)}, f32[336,1152]{1,0:T(8,128)S(1)}, u32[]{:S(2)}) copy-start(f32[336,1152]{1,0:T(8,128)S(1)} %get-tuple-element.111) | copy-start | bytes 4644868
  61.6 23.4 %copy-start.14 = (f32[336,4608]{1,0:T(8,128)}, f32[336,4608]{1,0:T(8,128)S(1)}, u32[]{:S(2)}) copy-start(f32[336,4608]{1,0:T(8,128)S(1)} %convolution_add_fusion) | copy-start | bytes 18579460
  131.0 15.8 %slice-start.4 = ((s8[6193152]{0:T(1024)(128)(4,1)}), s8[4194304]{0:T(1024)(128)(4,1)S(1)}, s32[]{:S(2)}) async-start(s8[6193152]{0:T(1024)(128)(4,1)} %bitcast.132), calls=%async_computation.4 | async-start | bytes 8388608
  157.8 53.9 %collective-permute-start.2 = (bf16[168,1152]{1,0:T(8,128)(2,1)}, bf16[168,1152]{1,0:T(8,128)(2,1)}, u32[]{:S(2)}, u32[]{:S(2)}) collective-permute-start(bf16[168,1152]{1,0:T(8,128)(2,1)} %get-tuple-element.84), channel_id=1, source_target_pairs={{0,1},{1,0},{2,3},{3,2},{4,5},{5,4},{6,7},{7,6},{8,9},{9,8},{10,11... | collective-permute-start | bytes 1161224 | tf_op jit(solution)/shard_map/ppermute | solution.py:40
  159.8 55.9 %collective-permute-start.5 = (bf16[336,576]{1,0:T(8,128)(2,1)}, bf16[336,576]{1,0:T(8,128)(2,1)}, u32[]{:S(2)}, u32[]{:S(2)}) collective-permute-start(bf16[336,576]{1,0:T(8,128)(2,1)} %select_convert_fusion), channel_id=1, source_target_pairs={{0,1},{1,0},{2,3},{3,2},{4,5},{5,4},{6,7},{7,6},{8,9},{9,8},{10,11... | collective-permute-start | bytes 1161224 | tf_op jit(solution)/shard_map/ppermute | solution.py:40
  172.8 43.1 %collective-permute-start.11 = (bf16[384,1152]{1,0:T(8,128)(2,1)}, bf16[384,1152]{1,0:T(8,128)(2,1)}, u32[]{:S(2)}, u32[]{:S(2)}) collective-permute-start(bf16[384,1152]{1,0:T(8,128)(2,1)} %pad.43.refs_10_), channel_id=1, source_target_pairs={{0,2},{2,0},{4,6},{6,4},{8,10},{10,8},{12,14},{14,12},{16,18},{18,... | collective-permute-start | bytes 2654216 | tf_op jit(solution)/shard_map/ppermute | solution.py:45
  172.9 59.1 %collective-permute-start.12 = (bf16[384,4608]{1,0:T(8,128)(2,1)S(1)}, bf16[384,4608]{1,0:T(8,128)(2,1)}, u32[]{:S(2)}, u32[]{:S(2)}) collective-permute-start(bf16[384,4608]{1,0:T(8,128)(2,1)S(1)} %copy-done), channel_id=1, source_target_pairs={{0,2},{2,0},{4,6},{6,4},{8,10},{10,8},{12,14},{14,12},{16,18},{18,... | collective-permute-start | bytes 10616840 | tf_op jit(solution)/shard_map/ppermute | solution.py:45
  191.2 24.0 %collective-permute-start.4 = (bf16[168,1152]{1,0:T(8,128)(2,1)}, bf16[168,1152]{1,0:T(8,128)(2,1)}, u32[]{:S(2)}, u32[]{:S(2)}) collective-permute-start(bf16[168,1152]{1,0:T(8,128)(2,1)} %select_convert_fusion.1), channel_id=1, source_target_pairs={{0,1},{1,0},{2,3},{3,2},{4,5},{5,4},{6,7},{7,6},{8,9},{9,8},{10,11... | collective-permute-start | bytes 1161224 | tf_op jit(solution)/shard_map/ppermute | solution.py:40
  211.6 4.8 %collective-permute-start.13 = (bf16[384,1152]{1,0:T(8,128)(2,1)S(1)}, bf16[384,1152]{1,0:T(8,128)(2,1)S(1)}, u32[]{:S(2)}, u32[]{:S(2)}) collective-permute-start(bf16[384,1152]{1,0:T(8,128)(2,1)S(1)} %copy-done.15), channel_id=1, source_target_pairs={{0,2},{2,0},{4,6},{6,4},{8,10},{10,8},{12,14},{14,12},{16,18},{18,... | collective-permute-start | bytes 2654216 | tf_op jit(solution)/shard_map/ppermute | solution.py:45
  215.2 16.8 %collective-permute-start.14 = (bf16[384,3456]{1,0:T(8,128)(2,1)S(1)}, bf16[384,3456]{1,0:T(8,128)(2,1)S(1)}, u32[]{:S(2)}, u32[]{:S(2)}) collective-permute-start(bf16[384,3456]{1,0:T(8,128)(2,1)S(1)} %copy-done.9), channel_id=1, source_target_pairs={{0,2},{2,0},{4,6},{6,4},{8,10},{10,8},{12,14},{14,12},{16,18},{18,... | collective-permute-start | bytes 7962632 | tf_op jit(solution)/shard_map/ppermute | solution.py:45
  215.7 7.2 %collective-permute-start.15 = (bf16[384,1152]{1,0:T(8,128)(2,1)}, bf16[384,1152]{1,0:T(8,128)(2,1)S(1)}, u32[]{:S(2)}, u32[]{:S(2)}) collective-permute-start(bf16[384,1152]{1,0:T(8,128)(2,1)} %pad.47.refs_18_), channel_id=1, source_target_pairs={{0,2},{2,0},{4,6},{6,4},{8,10},{10,8},{12,14},{14,12},{16,18},{18,... | collective-permute-start | bytes 2654216 | tf_op jit(solution)/shard_map/ppermute | solution.py:45
  215.9 9.6 %collective-permute-start.8 = (bf16[1280,384]{1,0:T(8,128)(2,1)S(1)}, bf16[1280,384]{1,0:T(8,128)(2,1)S(1)}, u32[]{:S(2)}, u32[]{:S(2)}) collective-permute-start(bf16[1280,384]{1,0:T(8,128)(2,1)S(1)} %get-tuple-element.79), channel_id=1, source_target_pairs={{0,2},{2,0},{4,6},{6,4},{8,10},{10,8},{12,14},{14,12},{16,18},{18,... | collective-permute-start | bytes 2949128 | tf_op jit(solution)/shard_map/ppermute | solution.py:45
  217.3 8.6 %collective-permute-start.9 = (bf16[1280,384]{1,0:T(8,128)(2,1)S(1)}, bf16[1280,384]{1,0:T(8,128)(2,1)S(1)}, u32[]{:S(2)}, u32[]{:S(2)}) collective-permute-start(bf16[1280,384]{1,0:T(8,128)(2,1)S(1)} %get-tuple-element.77), channel_id=1, source_target_pairs={{0,2},{2,0},{4,6},{6,4},{8,10},{10,8},{12,14},{14,12},{16,18},{18,... | collective-permute-start | bytes 2949128 | tf_op jit(solution)/shard_map/ppermute | solution.py:45
  222.9 9.0 %collective-permute-start.6 = (bf16[2304,384]{1,0:T(8,128)(2,1)S(1)}, bf16[2304,384]{1,0:T(8,128)(2,1)S(1)}, u32[]{:S(2)}, u32[]{:S(2)}) collective-permute-start(bf16[2304,384]{1,0:T(8,128)(2,1)S(1)} %get-tuple-element.71), channel_id=1, source_target_pairs={{0,2},{2,0},{4,6},{6,4},{8,10},{10,8},{12,14},{14,12},{16,18},{18,... | collective-permute-start | bytes 5308424 | tf_op jit(solution)/shard_map/ppermute | solution.py:45
  225.5 6.4 %collective-permute-start.7 = (bf16[1536,384]{1,0:T(8,128)(2,1)S(1)}, bf16[1536,384]{1,0:T(8,128)(2,1)S(1)}, u32[]{:S(2)}, u32[]{:S(2)}) collective-permute-start(bf16[1536,384]{1,0:T(8,128)(2,1)S(1)} %copy-done.34), channel_id=1, source_target_pairs={{0,2},{2,0},{4,6},{6,4},{8,10},{10,8},{12,14},{14,12},{16,18},{18,... | collective-permute-start | bytes 3538952 | tf_op jit(solution)/shard_map/ppermute | solution.py:45
  226.0 6.0 %collective-permute-start.10 = (bf16[1536,384]{1,0:T(8,128)(2,1)S(1)}, bf16[1536,384]{1,0:T(8,128)(2,1)S(1)}, u32[]{:S(2)}, u32[]{:S(2)}) collective-permute-start(bf16[1536,384]{1,0:T(8,128)(2,1)S(1)} %get-tuple-element.73), channel_id=1, source_target_pairs={{0,2},{2,0},{4,6},{6,4},{8,10},{10,8},{12,14},{14,12},{16,18},{18,... | collective-permute-start | bytes 3538952 | tf_op jit(solution)/shard_map/ppermute | solution.py:45
  421.3 13.4 %copy-start.46 = (f32[32,1152]{1,0:T(8,128)S(1)}, f32[32,1152]{1,0:T(8,128)}, u32[]{:S(2)}) copy-start(f32[32,1152]{1,0:T(8,128)} %get-tuple-element.44) | copy-start | bytes 442372
  421.3 13.4 %copy-start.47 = (f32[32,1152]{1,0:T(8,128)S(1)}, f32[32,1152]{1,0:T(8,128)}, u32[]{:S(2)}) copy-start(f32[32,1152]{1,0:T(8,128)} %get-tuple-element.45) | copy-start | bytes 442372
  421.3 13.3 %copy-start.48 = (f32[32,1152]{1,0:T(8,128)S(1)}, f32[32,1152]{1,0:T(8,128)}, u32[]{:S(2)}) copy-start(f32[32,1152]{1,0:T(8,128)} %get-tuple-element.46) | copy-start | bytes 442372
  421.3 13.3 %copy-start.49 = (f32[32,1152]{1,0:T(8,128)S(1)}, f32[32,1152]{1,0:T(8,128)}, u32[]{:S(2)}) copy-start(f32[32,1152]{1,0:T(8,128)} %get-tuple-element.47) | copy-start | bytes 442372
  (73 other events, 360.4 us)

commit v3 on v2

--- a/solution.py
+++ b/solution.py
@@ -1,8 +1,9 @@
 import functools
+import types
+import typing
 
 import jax
 import jax.numpy as jnp
-import numpy as np
 from jax import lax
 from jax.experimental import pallas as pl
 from jax.experimental.pallas import tpu as pltpu
@@ -55,8 +56,479 @@
     )
 
 
+PAD = 192
+ROWS = 2 * PAD
+
+
+def matmul_t(left, right):
+    return lax.dot_general(
+        left, right, (((1,), (1,)), ((), ())), preferred_element_type=jnp.float32
+    )
+
+
+def t_matmul(left, right):
+    return lax.dot_general(
+        left, right, (((0,), (0,)), ((), ())), preferred_element_type=jnp.float32
+    )
+
+
+def norm_parts(values):
+    center = values - jnp.mean(values, axis=-1, keepdims=True)
+    spread = jnp.mean(center * center, axis=-1, keepdims=True)
+    scale = lax.rsqrt(spread + epsilon)
+    return center * scale, scale
+
+
+def fold_rows(values):
+    rows, width = values.shape
+    return jnp.sum(values.reshape(rows // 8, 8, width), axis=0)
+
+
+def block_kernel(half, hidden, matrices, names, *refs):
+    r = types.SimpleNamespace(**dict(zip(names, refs)))
+    width = r.skip_weight.shape[1]
+    seq = lax.axis_index("seq")
+    core = lax.rem(lax.axis_index("dp"), 2)
+    sems = r.sems
+    low = jnp.bfloat16
+    counter = iter(range(64))
+
+    def copy(source, target):
+        return pltpu.make_async_copy(source, target, sems.at[next(counter)])
+
+    loads = types.SimpleNamespace(
+        in0=copy(r.inputs.at[seq], r.raw_in.at[seq]),
+        in1=copy(r.inputs_got, r.raw_in.at[1 - seq]),
+        sk0=copy(r.skipped.at[seq], r.raw_skip.at[seq]),
+        sk1=copy(r.skipped_got, r.raw_skip.at[1 - seq]),
+        skip0=copy(r.skip_weight.at[pl.ds(0, width), :], r.feed.at[0]),
+        skip1=copy(r.skip_weight.at[pl.ds(width, width), :], r.feed.at[1]),
+        ct0=copy(r.cotangent.at[seq], r.raw_out.at[seq]),
+        ct1=copy(r.cotangent_got, r.raw_out.at[1 - seq]),
+        qkv=copy(r.qkv_weight, r.qkv_buffer),
+        proj=copy(r.proj_weight, r.proj_buffer),
+    )
+    for load in vars(loads).values():
+        load.start()
+    chunk, feed = width, r.feed
+    feeds = []
+    for j in range(hidden // chunk):
+        part = pl.ds(j * chunk, chunk)
+        at = 2 - 2 * (j % 2)
+        feeds.append(
+            (
+                copy(r.fc1_weight.at[:, part], feed.at[at]),
+                copy(r.fc2_weight.at[part, :], feed.at[at + 1]),
+            )
+        )
+
+    def start(copies):
+        for item in copies:
+            item.start()
+
+    start(feeds[0])
+    stores = {}
+
+    def store(source, target):
+        item = copy(source, target)
+        item.start()
+        stores[id(item)] = item
+        return item
+
+    def finish(item):
+        stores.pop(id(item)).wait()
+
+    joined, skips, grad_out = r.joined, r.skips, r.grad_out
+    gap = PAD - half
+    for load in (loads.in0, loads.in1, loads.sk0, loads.sk1):
+        load.wait()
+    for h in range(2):
+        joined[pl.ds(h * PAD, PAD), :] = jnp.concatenate(
+            [r.raw_in[h], jnp.zeros((gap, width), low)], axis=0
+        )
+        for f in range(2):
+            skips[f, pl.ds(h * PAD, PAD), :] = jnp.concatenate(
+                [r.raw_skip[f, h], jnp.zeros((gap, width // 2), low)], axis=0
+            )
+    loads.skip0.wait()
+    loads.skip1.wait()
+    stream, tile = r.stream, 384
+
+    @pl.loop(0, width // tile)
+    def _(j):
+        columns = pl.ds(pl.multiple_of(j * tile, 128), tile)
+        total = matmul(joined[...], feed[0, :, columns])
+        total += matmul(skips[0], feed[1, pl.ds(0, width // 2), columns])
+        total += matmul(skips[1], feed[1, pl.ds(width // 2, width // 2), columns])
+        stream[:, columns] = total + r.skip_bias[:, columns]
+
+    start(feeds[1])
+    step = 32
+
+    def norm(source, gain, shift, target):
+        @pl.loop(0, ROWS // step)
+        def _(i):
+            rows = pl.ds(pl.multiple_of(i * step, step), step)
+            unit, _ = norm_parts(source[rows, :])
+            target[rows, :] = (unit * gain[...] + shift[...]).astype(low)
+
+    normed, packed = r.normed, r.packed
+    norm(stream, r.gain_one, r.shift_one, normed)
+    loads.qkv.wait()
+
+    @pl.loop(0, 3 * width // tile)
+    def _(j):
+        columns = pl.ds(pl.multiple_of(j * tile, 128), tile)
+        packed[:, columns] = matmul(normed[...], r.qkv_buffer[:, columns]).astype(low)
+
+    length = r.lengths[seq]
+    at = lax.broadcasted_iota(jnp.int32, (1, ROWS), 1)
+    inner = jnp.where(at >= PAD, at - PAD, at)
+    position = jnp.where(at >= PAD, at - PAD + half, at)
+    valid = (position == 0) | ((position >= 1) & (position <= length))
+    valid = valid | ((position >= 1 + CAPTION) & (position < 1 + CAPTION + IMAGE))
+    valid = valid & (inner < half)
+    scale = HEAD_DIM ** (-0.5)
+    window = 256
+
+    def head_window(h):
+        start = jnp.minimum(lax.div(h * HEAD_DIM, 128) * 128, width - window)
+        start = pl.multiple_of(start, 128)
+        lane = lax.broadcasted_iota(jnp.int32, (1, window), 1) + start
+        mine = (lane >= h * HEAD_DIM) & (lane < (h + 1) * HEAD_DIM)
+        return start, mine
+
+    def part(which, start):
+        return packed[:, pl.ds(pl.multiple_of(which * width + start, 128), window)]
+
+    mixed_sum, probs = r.sum_a, r.probs
+
+    def attend(h, carry):
+        start, mine = head_window(h)
+        query = jnp.where(mine, part(0, start), jnp.zeros((), low))
+        scores = matmul_t(query, part(1, start)) * scale
+        scores = jnp.where(valid, scores, masked_score)
+        expo = jnp.exp(scores - jnp.max(scores, axis=-1, keepdims=True))
+        share = expo * (1.0 / jnp.sum(expo, axis=-1, keepdims=True))
+        share = share.astype(low)
+        probs[h] = share
+        found = matmul(share, part(2, start))
+        columns = pl.ds(start, window)
+        mixed_sum[:, columns] = jnp.where(mine, found, mixed_sum[:, columns])
+        return carry
+
+    lax.fori_loop(0, HEADS, attend, 0, unroll=2)
+    mixed, stream_two = r.mixed, r.stream_two
+    mixed[...] = mixed_sum[...].astype(low)
+    loads.proj.wait()
+
+    @pl.loop(0, width // tile)
+    def _(j):
+        columns = pl.ds(pl.multiple_of(j * tile, 128), tile)
+        total = matmul(mixed[...], r.proj_buffer[:, columns]) + r.proj_bias[:, columns]
+        stream_two[:, columns] = stream[:, columns] + total
+
+    normed_two = r.normed_two
+    norm(stream_two, r.gain_two, r.shift_two, normed_two)
+    for load in (loads.ct0, loads.ct1):
+        load.wait()
+    for h in range(2):
+        grad_out[pl.ds(h * PAD, PAD), :] = jnp.concatenate(
+            [r.raw_out[h], jnp.zeros((gap, width), low)], axis=0
+        )
+    store(grad_out, r.right_fc2)
+    sums = r.sums
+    sums[7:8, :] = jnp.sum(grad_out[...].astype(jnp.float32), axis=0, keepdims=True)
+
+    forward, backward = r.sum_a, r.sum_b
+    acted, grad_hidden, staged = r.acted, r.grad_hidden, r.left_fc2_stage
+    pending = {}
+    for j, loading in enumerate(feeds):
+        slot = j % 2
+        first, second = feed.at[2 - 2 * slot], feed.at[3 - 2 * slot]
+        for load in loading:
+            load.wait()
+        for item in pending.get(slot, ()):
+            finish(item)
+
+        @pl.loop(0, chunk // tile)
+        def _(t):
+            columns = pl.ds(pl.multiple_of(t * tile, 128), tile)
+            whole = pl.ds(pl.multiple_of(j * chunk + t * tile, 128), tile)
+            value = matmul(normed_two[...], first[:, columns])
+            value += r.fc1_bias[:, whole]
+            phi = 0.5 + 0.5 * lax.erf(value * (0.5**0.5))
+            bell = jnp.exp(-0.5 * value * value) * ((2 * jnp.pi) ** -0.5)
+            acted[slot, :, columns] = (value * phi).astype(low)
+            back = matmul_t(grad_out[...], second[columns, :])
+            back = (back * (phi + value * bell)).astype(low)
+            grad_hidden[slot, :, columns] = back
+            sums[pl.ds(8 + j, 1), columns] = jnp.sum(
+                back.astype(jnp.float32), axis=0, keepdims=True
+            )
+
+        @pl.loop(0, width // tile)
+        def _(t):
+            columns = pl.ds(pl.multiple_of(t * tile, 128), tile)
+            ahead = matmul(acted[slot], second[:, columns])
+            back = matmul_t(grad_hidden[slot], first[columns, :])
+            if j == 0:
+                forward[:, columns] = ahead
+                backward[:, columns] = back
+            else:
+                forward[:, columns] += ahead
+                backward[:, columns] += back
+
+        share = matrices[0].share
+        turned = acted[slot].T
+        groups = chunk // (4 * share)
+        for g in range(groups):
+            for c in range(2):
+                begin = (g * 2 + c) * 2 * share
+                staged[slot, c ^ core, pl.ds(g * 2 * share, 2 * share), :] = turned[
+                    begin : begin + 2 * share
+                ]
+        count = groups * 2 * share
+        pending[slot] = [
+            store(staged.at[slot], r.left_fc2.at[:, pl.ds(j * count, count), :]),
+            store(grad_hidden.at[slot], r.right_fc1.at[:, pl.ds(j * chunk, chunk)]),
+        ]
+        if j + 2 < len(feeds):
+            start(feeds[j + 2])
+        elif slot == 0:
+            again = [copy(r.skip_weight.at[pl.ds(k * width, width), :], feed.at[2 + k]) for k in range(2)]
+            start(again)
+
+    turned_ref = r.turned
+    stages = {}
+
+    def left(m, target, sources):
+        matrix = matrices[m]
+        stage = r.left_stage
+        if stages:
+            finish(stages.pop(0))
+        share, main, rest = matrix.share, matrix.main, matrix.rest
+        folds, body = len(matrix.pieces), 16 * main
+        first = 0
+        for source in sources:
+            turned_ref[pl.ds(32, width), :] = source.astype(jnp.float32).T
+            for k in range(width // share):
+                number = first + k
+                c, block = number // 2 % 2, number // 4 * 2 + number % 2
+                base = 32 + k * share
+                place = c ^ core
+                stage[place, pl.ds(block * main, main), :] = turned_ref[
+                    pl.ds(base, main), :
+                ].astype(low)
+                row = lax.broadcasted_iota(jnp.int32, (16, 1), 0)
+                for q in range(folds):
+                    part = turned_ref[pl.ds(base + main - q * rest, 16), :]
+                    part = jnp.where((row >= q * rest) & (row < (q + 1) * rest), part, 0.0)
+                    stage[place, pl.ds(body + (q * 16 + block) * 16, 16), :] = part.astype(low)
+            first += width // share
+        rows = matrix.left_rows(16)
+        stages[0] = store(stage.at[:, pl.ds(0, rows), :], target)
+
+    left(1, r.left_fc1, [normed_two[...]])
+    left(2, r.left_proj, [mixed[...]])
+    left(3, r.left_qkv, [normed[...]])
+    left(4, r.left_skip, [joined[...], jnp.concatenate([skips[0], skips[1]], axis=1)])
+
+    grad_two = r.grad_two
+    out_stage, grad_low = r.out_stage, r.grad_low
+    for h in range(2):
+        rows = pl.ds(h * PAD, half)
+        value = stream_two[rows, :] + (forward[rows, :] + r.fc2_bias[...])
+        out_stage[h] = value.astype(low)
+    store(out_stage.at[seq], r.block_own)
+    store(out_stage.at[1 - seq], r.block_send)
+
+    def norm_back(source, gain, back, extra, target, target_low, gain_row, shift_row):
+        partial = r.partial
+        partial[...] = jnp.zeros_like(partial)
+
+        @pl.loop(0, ROWS // step)
+        def _(i):
+            rows = pl.ds(pl.multiple_of(i * step, step), step)
+            unit, spread = norm_parts(source[rows, :])
+            value = back[rows, :]
+            partial[0] += fold_rows(value * unit)
+            partial[1] += fold_rows(value)
+            value = value * gain[...]
+            mean = jnp.mean(value, axis=-1, keepdims=True)
+            slope = jnp.mean(value * unit, axis=-1, keepdims=True)
+            value = spread * (value - mean - unit * slope)
+            value = value + extra[rows, :].astype(jnp.float32)
+            if target is not None:
+                target[rows, :] = value
+            rounded = value.astype(low)
+            target_low[rows, :] = rounded
+            partial[2] += fold_rows(rounded.astype(jnp.float32))
+
+        sums[gain_row : gain_row + 1, :] = jnp.sum(partial[0], axis=0, keepdims=True)
+        sums[shift_row : shift_row + 1, :] = jnp.sum(partial[1], axis=0, keepdims=True)
+        return jnp.sum(partial[2], axis=0, keepdims=True)
+
+    sums[3:4, :] = norm_back(stream_two, r.gain_two, backward, grad_out, grad_two, grad_low, 4, 5)
+    store(grad_low, r.right_proj)
+    grad_mixed = r.grad_mixed
+
+    @pl.loop(0, width // tile)
+    def _(j):
+        columns = pl.ds(pl.multiple_of(j * tile, 128), tile)
+        grad_mixed[:, columns] = matmul_t(grad_low[...], r.proj_buffer[columns, :]).astype(low)
+
+    grad_query, grad_key, grad_value = r.sum_a, r.sum_b, r.sum_c
+
+    def attend_back(h, carry):
+        start, mine = head_window(h)
+        zero = jnp.zeros((), low)
+        columns = pl.ds(start, window)
+        query = jnp.where(mine, part(0, start), zero)
+        back = jnp.where(mine, grad_mixed[:, columns], zero)
+        share = probs[h]
+        grad_share = matmul_t(back, part(2, start))
+        wide = share.astype(jnp.float32)
+        level = jnp.sum(wide * grad_share, axis=-1, keepdims=True)
+        grad_score = (wide * (grad_share - level)).astype(low)
+        found = t_matmul(share, back)
+        grad_value[:, columns] = jnp.where(mine, found, grad_value[:, columns])
+        found = matmul(grad_score, part(1, start)) * scale
+        grad_query[:, columns] = jnp.where(mine, found, grad_query[:, columns])
+        found = t_matmul(grad_score, query) * scale
+        grad_key[:, columns] = jnp.where(mine, found, grad_key[:, columns])
+        return carry
+
+    lax.fori_loop(0, HEADS, attend_back, 0, unroll=2)
+    for k, source in enumerate((grad_query, grad_key, grad_value)):
+        packed[:, pl.ds(k * width, width)] = source[...].astype(low)
+    store(packed, r.right_qkv)
+    grad_normed = r.sum_a
+
+    @pl.loop(0, width // tile)
+    def _(j):
+        columns = pl.ds(pl.multiple_of(j * tile, 128), tile)
+        grad_normed[:, columns] = matmul_t(packed[...], r.qkv_buffer[columns, :])
+
+    grad_stream = r.grad_mixed
+    sums[0:1, :] = norm_back(stream, r.gain_one, grad_normed, grad_two, None, grad_stream, 1, 2)
+    store(grad_stream, r.right_skip)
+    sums[12:16, :] = jnp.zeros((4, width), jnp.float32)
+    sums[6:7, :] = jnp.zeros((1, width), jnp.float32)
+    store(sums, r.vectors)
+
+    back_in = r.sum_b
+    for load in again:
+        load.wait()
+
+    @pl.loop(0, width // tile)
+    def _(j):
+        columns = pl.ds(pl.multiple_of(j * tile, 128), tile)
+        back_in[:, columns] = matmul_t(grad_stream[...], feed[2, columns, :])
+
+    store(back_in.at[pl.ds(pl.multiple_of(seq * PAD, 64), half), :], r.grad_in_own)
+    send_in = r.send_in
+    send_in[...] = back_in[pl.ds(pl.multiple_of((1 - seq) * PAD, 64), half), :].astype(low)
+    store(send_in, r.grad_in_send)
+    feature = width // 2
+    for f in range(2):
+        value = matmul_t(grad_stream[...], feed[3, pl.ds(f * feature, feature), :])
+        for h in range(2):
+            piece = value[h * PAD : h * PAD + half]
+
+            @pl.when(seq == f)
+            def _():
+                r.own_skip[h] = piece
+
+            @pl.when(seq != f)
+            def _():
+                r.send_skip[h] = piece.astype(low)
+
+    store(r.own_skip, r.grad_skip_own)
+    store(r.send_skip, r.grad_skip_send)
+    for item in stores.values():
+        item.wait()
+
+
+LEFTS = ["left_fc2", "left_fc1", "left_proj", "left_qkv", "left_skip"]
+RIGHTS = ["right_fc2", "right_fc1", "right_proj", "right_qkv", "right_skip"]
+
+
+def run_block(arrays, matrices, width, hidden, half):
+    low, wide = jnp.bfloat16, jnp.float32
+    shape = jax.ShapeDtypeStruct
+    outs = dict(
+        block_own=shape((half, width), low),
+        block_send=shape((half, width), low),
+        grad_in_own=shape((half, width), wide),
+        grad_in_send=shape((half, width), low),
+        grad_skip_own=shape((2, half, width // 2), wide),
+        grad_skip_send=shape((2, half, width // 2), low),
+        vectors=shape((16, width), wide),
+    )
+    lefts = [shape((2, matrix.left_rows(16), ROWS), low) for matrix in matrices]
+    rights = [shape((ROWS, matrix.columns), low) for matrix in matrices]
+    outs.update(zip(LEFTS, lefts))
+    outs.update(zip(RIGHTS, rights))
+    staged = 16 * matrices[0].share // (hidden // width)
+    square = (ROWS, width)
+    scratch = dict(
+        raw_in=((2, half, width), low),
+        raw_skip=((2, 2, half, width // 2), low),
+        raw_out=((2, half, width), low),
+        qkv_buffer=((width, 3 * width), low),
+        proj_buffer=((width, width), low),
+        feed=((4, width, width), low),
+        joined=(square, low),
+        skips=((2, ROWS, width // 2), low),
+        grad_out=(square, low),
+        stream=(square, wide),
+        normed=(square, low),
+        packed=((ROWS, 3 * width), low),
+        probs=((HEADS, ROWS, ROWS), low),
+        sum_a=(square, wide),
+        sum_b=(square, wide),
+        sum_c=(square, wide),
+        mixed=(square, low),
+        stream_two=(square, wide),
+        normed_two=(square, low),
+        acted=((2,) + square, low),
+        grad_hidden=((2,) + square, low),
+        left_fc2_stage=((2, 2, staged, ROWS), low),
+        left_stage=((2, max(m.left_rows(16) for m in matrices[1:]), ROWS), low),
+        turned=((width + 64, ROWS), wide),
+        sums=((16, width), wide),
+        partial=((3, 8, width), wide),
+        grad_two=(square, wide),
+        out_stage=((2, half, width), low),
+        grad_low=(square, low),
+        grad_mixed=(square, low),
+        send_in=((half, width), low),
+        own_skip=((2, half, width // 2), wide),
+        send_skip=((2, half, width // 2), low),
+    )
+    anywhere = pl.BlockSpec(memory_space=pl.ANY)
+    vmem = pl.BlockSpec(memory_space=pltpu.VMEM)
+    smem = pl.BlockSpec(memory_space=pltpu.SMEM)
+    small = {name for name, a in arrays.items() if a.dtype == wide}
+    specs = [smem if n == "lengths" else vmem if n in small else anywhere for n in arrays]
+    names = list(arrays) + list(outs) + list(scratch) + ["sems"]
+    results = pl.pallas_call(
+        functools.partial(block_kernel, half, hidden, matrices, names),
+        out_shape=list(outs.values()),
+        in_specs=specs,
+        out_specs=[anywhere] * len(outs),
+        scratch_shapes=[pltpu.VMEM(*s) for s in scratch.values()]
+        + [pltpu.SemaphoreType.DMA((64,))],
+        compiler_params=pltpu.CompilerParams(vmem_limit_bytes=63 * 2**20),
+        name="block",
+    )(*arrays.values())
+    return types.SimpleNamespace(**dict(zip(outs, results)))
+
+
 MESH = pl.DeviceIdType.MESH
 LANES = 384
+SHIPS = 3
 TWO = 2 * LANES
 
 
@@ -96,21 +568,23 @@
 
 def reduce_kernel(matrices, units, events, dims, *refs):
     count = len(matrices)
-    lefts = [(refs[2 * i], refs[2 * i + 1]) for i in range(count)]
-    refs = refs[2 * count :]
-    rights = [(refs[2 * i], refs[2 * i + 1]) for i in range(count)]
-    refs = refs[2 * count :]
+    lefts, refs = refs[:count], refs[count:]
+    rights, refs = refs[:count], refs[count:]
     vector_ref, refs = refs[0], refs[1:]
+    ships, refs = refs[:SHIPS], refs[SHIPS:]
     outs, refs = refs[: len(units)], refs[len(units) :]
+    docks, refs = refs[:SHIPS], refs[SHIPS:]
+    far_lefts, refs = refs[:count], refs[count:]
+    far_rights, refs = refs[:count], refs[count:]
     vector_out, refs = refs[0], refs[1:]
     grads, refs = refs[: len(units)], refs[len(units) :]
     hops = len(dims)
     landed = [refs[i * hops : (i + 1) * hops] for i in range(len(units))]
     refs = refs[len(units) * hops :]
-    vector_land, refs = refs[: hops + 1], refs[hops + 1 :]
-    vector_sum, refs = refs[0], refs[1:]
+    vector_land, vector_sum, refs = refs[0], refs[1], refs[2:]
     fold_sum, left_buffer, right_buffer, refs = refs[0], refs[1], refs[2], refs[3:]
-    send_sem, recv_sem, vsend_sem, vrecv_sem, left_sem, right_sem = refs
+    send_sem, recv_sem, vsend_sem, vrecv_sem, left_sem, right_sem, *refs = refs
+    xsend_sem, xrecv_sem, ship_send, ship_recv = refs
 
     dp = lax.axis_index("dp")
     seq = lax.axis_index("seq")
@@ -129,11 +603,41 @@
         pl.semaphore_signal(barrier, inc=1, device_id=partner(name), device_id_type=MESH)
     pl.semaphore_wait(barrier, len(dims) + 1)
 
+    sent = []
+
+    def remote(source, target, send_at, recv_at, name):
+        copy = pltpu.make_async_remote_copy(
+            src_ref=source,
+            dst_ref=target,
+            send_sem=send_at,
+            recv_sem=recv_at,
+            device_id=partner(name),
+            device_id_type=MESH,
+        )
+        copy.start()
+        sent.append(copy)
+        return copy
+
+    crossing = {}
+    for m in range(count):
+        crossing[m] = [
+            remote(lefts[m].at[1], far_lefts[m], xsend_sem.at[m, 0], xrecv_sem.at[m, 0], 0),
+            remote(rights[m], far_rights[m], xsend_sem.at[m, 1], xrecv_sem.at[m, 1], 0),
+        ]
+    arrived = set()
+
+    def meet(m):
+        if m not in arrived:
+            arrived.add(m)
+            for copy in crossing[m]:
+                copy.wait_recv()
+
     def left_copies(m):
+        meet(m)
         rows = matrices[m].left_rows(2 ** len(dims))
         return [
             pltpu.make_async_copy(
-                lefts[m][k],
+                (lefts[m].at[0], far_lefts[m])[k],
                 left_buffer.at[m % 2, pl.ds(0, rows), pl.ds(k * LANES, LANES)],
                 left_sem.at[m % 2, k],
             )
@@ -144,10 +648,11 @@
 
     def right_copies(index):
         m, p = all_pieces[index]
+        meet(m)
         start, width = matrices[m].pieces[p]
         return [
             pltpu.make_async_copy(
-                rights[m][k].at[:, pl.ds(start, width)],
+                (rights[m], far_rights[m])[k].at[:, pl.ds(start, width)],
                 right_buffer.at[index % 2, pl.ds(k * LANES, LANES), pl.ds(0, width)],
                 right_sem.at[index % 2, k],
             )
@@ -162,12 +667,10 @@
         for copy in copies:
             copy.wait()
 
-    for m in range(2):
-        start(left_copies(m))
+    start(left_copies(0))
     for index in range(2):
         start(right_copies(index))
-
-    sent = []
+    start(left_copies(1))
 
     def send(u, h):
         unit = units[u]
@@ -179,17 +682,13 @@
                 index.append(1 - bit(name))
             else:
                 index.append(slice(None))
-        copy = pltpu.make_async_remote_copy(
-            src_ref=grads[u].at[tuple(index)],
-            dst_ref=landed[u][h],
-            send_sem=send_sem.at[u, h],
-            recv_sem=recv_sem.at[u, h],
-            device_id=partner(unit.hops[h]),
-            device_id_type=MESH,
+        return remote(
+            grads[u].at[tuple(index)],
+            landed[u][h],
+            send_sem.at[u, h],
+            recv_sem.at[u, h],
+            unit.hops[h],
         )
-        copy.start()
-        sent.append(copy)
-        return copy
 
     flying = {}
 
@@ -216,9 +715,6 @@
                 outs[u][rows] = total
             else:
                 grads[u][own] = total.astype(jnp.bfloat16)
-
-        if not last:
-            flying[u, h + 1] = send(u, h + 1)
 
     def multiply(index):
         m, p = all_pieces[index]
@@ -276,52 +772,46 @@
         last = p + 1 == len(matrix.pieces)
         if last and m + 2 < count:
             start(left_copies(m + 2))
-        if start_column + width == units[u].start + units[u].columns:
-            flying[u, 0] = send(u, 0)
         if last and matrix.rest:
             f = next(i for i, unit in enumerate(units) if unit.matrix == m and unit.folded)
             folded = fold_sum[:, pl.ds(0, units[f].columns)].astype(jnp.bfloat16)
             grads[f][...] = folded.reshape((2,) * len(dims) + (16, units[f].columns))
-            flying[f, 0] = send(f, 0)
+
+    shipped = {}
+
+    def ship(k):
+        return remote(ships[k], docks[k], ship_send.at[k], ship_recv.at[k], "seq")
+
+    path = [0] + list(dims)
+    vector_flying = {}
 
     def vector_send(h):
-        name = 0 if h == 0 else dims[h - 1]
-        source = vector_ref.at[1 - core] if h == 0 else vector_sum.at[
-            tuple(bit(n) for n in dims[: h - 1]) + (1 - bit(name),)
-        ]
-        copy = pltpu.make_async_remote_copy(
-            src_ref=source,
-            dst_ref=vector_land[h],
-            send_sem=vsend_sem.at[h],
-            recv_sem=vrecv_sem.at[h],
-            device_id=partner(name),
-            device_id_type=MESH,
-        )
-        copy.start()
-        sent.append(copy)
-        return copy
-
-    vector_flying = {}
+        source = vector_ref if h == 0 else vector_sum.at[h - 1]
+        return remote(source, vector_land.at[h], vsend_sem.at[h], vrecv_sem.at[h], path[h])
 
     def vector_add(h):
         vector_flying[h].wait_recv()
-        own = tuple(bit(n) for n in dims[:h])
-        if h == 0:
-            vector_sum[...] = vector_ref[core] + vector_land[0][...]
-        elif h < hops:
-            vector_sum[own] = vector_sum[own] + vector_land[h][...]
+        before = vector_ref[...] if h == 0 else vector_sum[h - 1]
+        total = before + vector_land[h]
+        if h < hops:
+            vector_sum[h] = total
+            vector_flying[h + 1] = vector_send(h + 1)
         else:
-            vector_out[...] = vector_sum[own] + vector_land[h][...]
-        if h < hops:
-            vector_flying[h + 1] = vector_send(h + 1)
+            vector_out[...] = total
 
     vector_flying[0] = vector_send(0)
     vector_done, since = 0, 0
-    for event in events:
-        if event[0] == "c":
-            multiply(event[1])
+    for action, u, h in events:
+        if action == COMPUTE:
+            multiply(u)
+        elif action == SEND and u == SHIP:
+            shipped[h] = ship(h)
+        elif action == SEND:
+            flying[u, h] = send(u, h)
+        elif u == SHIP:
+            shipped[h].wait_recv()
         else:
-            add(*event)
+            add(u, h)
             since += 1
             if since % 4 == 0 and vector_done <= hops:
                 vector_add(vector_done)
@@ -333,79 +823,63 @@
         copy.wait_send()
 
 
-def left_operand(values, matrix, blocks, core_count):
-    rows, depth = values.shape
-    padded = jnp.pad(values, ((0, LANES - rows), (0, 0)))
-    if not matrix.rest:
-        parts = padded.T.reshape(blocks // 2, core_count, 2, matrix.share, LANES)
-        return parts.transpose(1, 0, 2, 3, 4).reshape(core_count, -1, LANES)
-    folds = len(matrix.pieces)
-    size = matrix.left_rows(blocks)
-    row = np.arange(core_count * size)
-    at_core, at = row // size, row % size
-    body = at < blocks * matrix.main
-    fold_at = np.maximum(at - blocks * matrix.main, 0)
-    piece, fold_row = fold_at // (blocks * 16), fold_at % (blocks * 16)
-    block = np.where(body, at // max(matrix.main, 1), fold_row // 16)
-    inner = np.where(body, at % max(matrix.main, 1), matrix.main + fold_row % 16 - piece * matrix.rest)
-    inside = body | ((fold_row % 16 >= piece * matrix.rest) & (fold_row % 16 < (piece + 1) * matrix.rest))
-    column = ((block // 2 * core_count + at_core) * 2 + block % 2) * matrix.share + inner
-    column = jnp.asarray(np.where(inside, column, -1), jnp.int32)
-    choose = (column[:, None] == jnp.arange(depth, dtype=jnp.int32)[None, :]).astype(jnp.bfloat16)
-    picked = lax.dot_general(
-        choose, padded, (((1,), (1,)), ((), ())), preferred_element_type=jnp.float32
-    )
-    return picked.astype(jnp.bfloat16).reshape(core_count, size, LANES)
-
-
-HOPS = {
-    "xyz": ("seq", 1, 2, 3),
-    "yxz": (1, "seq", 2, 3),
-    "yzx": (1, 2, 3, "seq"),
-    "zxy": (2, 3, "seq", 1),
-    "zyx": (2, 3, 1, "seq"),
-    "xzy": ("seq", 2, 3, 1),
-}
-HOP_PLAN = ["xyz", "zxy", "yzx", "yzx", "xyz", "xyz", "zyx", "yxz", "xyz", "yxz", "xyz", "xyz", "xyz", "xyz", "yzx", "xyz", "xzy"]
+X, Y, Z, ZZ = "seq", 1, 2, 3
+XYZ, YXZ, YZX = (X, Y, Z, ZZ), (Y, X, Z, ZZ), (Y, Z, ZZ, X)
+ZXY, ZYX, XZY = (Z, ZZ, X, Y), (Z, ZZ, Y, X), (X, Z, ZZ, Y)
+COMPUTE, SEND, TAKE, SHIP = 0, 1, 2, -1
+HOP_PLAN = [YXZ, ZYX, YXZ, XYZ, XYZ, ZXY, YXZ, ZXY, YZX, XZY, YXZ, YXZ, XZY, XYZ, YXZ, XZY, XYZ]
 EVENTS = [
-    ("c", 0), ("c", 1), ("c", 2), ("c", 3), ("c", 4), ("c", 5), ("c", 6), ("c", 7), ("c", 8),
-    ("c", 9), ("c", 10), (0, 0), (1, 0), ("c", 11), (2, 0), ("c", 12), ("c", 13), (4, 0),
-    ("c", 14), (6, 0), (3, 0), (5, 0), (7, 0), (9, 0), (1, 1), (2, 1), (0, 1), (8, 0), (6, 1),
-    (3, 1), (10, 0), (2, 2), (14, 0), (0, 2), (3, 2), (4, 1), (11, 0), (5, 1), (0, 3), (14, 1),
-    (8, 1), (4, 2), (6, 2), (5, 2), (12, 0), (14, 2), (10, 1), (4, 3), (13, 0), (8, 2), (5, 3),
-    (11, 1), (8, 3), (10, 2), (12, 1), (15, 0), (11, 2), (10, 3), (13, 1), (16, 0), (12, 2),
-    (11, 3), (7, 1), (9, 1), (13, 2), (15, 1), (16, 1), (12, 3), (13, 3), (1, 2), (7, 2), (9, 2),
-    (16, 2), (2, 3), (3, 3), (15, 2), (1, 3), (7, 3), (16, 3), (6, 3), (9, 3), (14, 3), (15, 3),
+    (SEND, SHIP, 0), (SEND, SHIP, 1), (COMPUTE, 0, 0), (SEND, 0, 0), (COMPUTE, 1, 0),
+    (SEND, 1, 0), (COMPUTE, 2, 0), (SEND, 2, 0), (COMPUTE, 3, 0), (TAKE, SHIP, 0), (SEND, 3, 0),
+    (COMPUTE, 4, 0), (COMPUTE, 5, 0), (SEND, 5, 0), (TAKE, SHIP, 1), (SEND, 4, 0),
+    (COMPUTE, 6, 0), (COMPUTE, 7, 0), (COMPUTE, 8, 0), (SEND, 6, 0), (TAKE, 0, 0),
+    (COMPUTE, 9, 0), (SEND, 7, 0), (TAKE, 1, 0), (SEND, 1, 1), (COMPUTE, 10, 0), (SEND, 0, 1),
+    (TAKE, 3, 0), (COMPUTE, 11, 0), (COMPUTE, 12, 0), (COMPUTE, 13, 0), (TAKE, 5, 0),
+    (SEND, 5, 1), (COMPUTE, 14, 0), (SEND, 14, 0), (TAKE, 2, 0), (SEND, 12, 0), (TAKE, 4, 0),
+    (TAKE, 7, 0), (SEND, 7, 1), (TAKE, 1, 1), (SEND, 15, 0), (TAKE, 0, 1), (SEND, 0, 2),
+    (SEND, 8, 0), (TAKE, 6, 0), (TAKE, 5, 1), (SEND, 2, 1), (TAKE, 12, 0), (SEND, 12, 1),
+    (TAKE, 7, 1), (SEND, 10, 0), (TAKE, 14, 0), (TAKE, 0, 2), (SEND, 0, 3), (SEND, 14, 1),
+    (TAKE, 15, 0), (SEND, 15, 1), (TAKE, 12, 1), (SEND, 12, 2), (TAKE, 0, 3), (SEND, 11, 0),
+    (TAKE, 8, 0), (SEND, 8, 1), (TAKE, 15, 1), (SEND, 15, 2), (SEND, 13, 0), (TAKE, 2, 1),
+    (SEND, 2, 2), (TAKE, 12, 2), (SEND, 6, 1), (TAKE, 14, 1), (TAKE, 15, 2), (SEND, 14, 2),
+    (TAKE, 8, 1), (SEND, 8, 2), (SEND, 3, 1), (TAKE, 10, 0), (SEND, 10, 1), (TAKE, 13, 0),
+    (TAKE, 2, 2), (SEND, 2, 3), (TAKE, 8, 2), (TAKE, 14, 2), (SEND, 14, 3), (SEND, 16, 0),
+    (TAKE, 6, 1), (SEND, 6, 2), (SEND, 4, 1), (TAKE, 11, 0), (TAKE, 2, 3), (SEND, 11, 1),
+    (TAKE, 10, 1), (SEND, 10, 2), (TAKE, 14, 3), (SEND, 1, 2), (TAKE, 3, 1), (SEND, 3, 2),
+    (SEND, 5, 2), (TAKE, 16, 0), (TAKE, 6, 2), (SEND, 6, 3), (TAKE, 10, 2), (SEND, 10, 3),
+    (SEND, 13, 1), (TAKE, 4, 1), (SEND, 4, 2), (SEND, 9, 0), (SEND, 7, 2), (SEND, 8, 3),
+    (TAKE, 11, 1), (SEND, 11, 2), (TAKE, 6, 3), (TAKE, 3, 2), (SEND, 3, 3), (SEND, 16, 1),
+    (SEND, 12, 3), (SEND, 15, 3), (TAKE, 1, 2), (SEND, 1, 3), (TAKE, 5, 2), (TAKE, 10, 3),
+    (SEND, SHIP, 2), (TAKE, 9, 0), (SEND, 9, 1), (SEND, 5, 3), (TAKE, 13, 1), (SEND, 13, 2),
+    (TAKE, 4, 2), (SEND, 4, 3), (TAKE, 3, 3), (TAKE, 7, 2), (SEND, 7, 3), (TAKE, 16, 1),
+    (SEND, 16, 2), (TAKE, 8, 3), (TAKE, 12, 3), (TAKE, 11, 2), (SEND, 11, 3), (TAKE, 15, 3),
+    (TAKE, 1, 3), (TAKE, 5, 3), (TAKE, 9, 1), (SEND, 9, 2), (TAKE, 4, 3), (TAKE, 7, 3),
+    (TAKE, 13, 2), (SEND, 13, 3), (TAKE, 11, 3), (TAKE, 16, 2), (SEND, 16, 3), (TAKE, 9, 2),
+    (SEND, 9, 3), (TAKE, 13, 3), (TAKE, SHIP, 2), (TAKE, 9, 3), (TAKE, 16, 3),
 ]
 
 
-def weight_gradients(pairs, lines, plan, bits):
+def weight_gradients(lefts, rights, vectors, ships, plan, bits):
     matrices, units, events = plan
     blocks = 2**bits
     dims = list(reversed(range(1, bits))) + ["seq"]
-    core = lax.axis_index("dp") & 1
-    operands = []
-    for (left, _), matrix in zip(pairs, matrices):
-        both = left_operand(left, matrix, blocks, 2)
-        operands += [pick(both, core, 0), swap_dp(pick(both, 1 - core, 0), 0)]
-    for _, right in pairs:
-        padded = jnp.pad(right, ((0, LANES - right.shape[0]), (0, 0)))
-        operands += [padded, swap_dp(padded, 0)]
-    operands.append(lines)
+    operands = [*lefts, *rights, vectors, *ships]
     anywhere = pl.BlockSpec(memory_space=pl.ANY)
     vmem = pl.BlockSpec(memory_space=pltpu.VMEM)
-    hops = len(dims)
-    outs = [jax.ShapeDtypeStruct((unit.rows, unit.columns), jnp.float32) for unit in units]
-    outs.append(jax.ShapeDtypeStruct(lines.shape[-2:], jnp.float32))
+    hops, count = len(dims), len(matrices)
+    shape = jax.ShapeDtypeStruct
+    outs = [shape((unit.rows, unit.columns), jnp.float32) for unit in units]
+    outs += [shape(ship.shape, ship.dtype) for ship in ships]
+    outs += [shape(left.shape[1:], left.dtype) for left in lefts]
+    outs += [shape(right.shape, right.dtype) for right in rights]
+    outs.append(shape(vectors.shape, jnp.float32))
     low = jnp.bfloat16
     scratch = [pltpu.VMEM((2,) * hops + (unit.rows, unit.columns), low) for unit in units]
     for unit in units:
         for h in range(hops):
             scratch.append(pltpu.VMEM((2,) * (hops - 1 - h) + (unit.rows, unit.columns), low))
-    tail = lines.shape[-2:]
-    for h in range(hops + 1):
-        scratch.append(pltpu.VMEM((2,) * (hops - h) + tail, jnp.float32))
-    scratch.append(pltpu.VMEM((2,) * hops + tail, jnp.float32))
+    scratch.append(pltpu.VMEM((hops + 1,) + vectors.shape, jnp.float32))
+    scratch.append(pltpu.VMEM((hops,) + vectors.shape, jnp.float32))
     folded = [matrix.fold_width for matrix in matrices if matrix.rest]
     scratch.append(pltpu.VMEM((blocks * 16, max(folded)), jnp.float32))
     scratch.append(pltpu.VMEM((2, max(m.left_rows(blocks) for m in matrices), TWO), low))
@@ -413,11 +887,13 @@
     scratch += [pltpu.SemaphoreType.DMA((len(units), hops))] * 2
     scratch += [pltpu.SemaphoreType.DMA((hops + 1,))] * 2
     scratch += [pltpu.SemaphoreType.DMA((2, 2))] * 2
+    scratch += [pltpu.SemaphoreType.DMA((count, 2))] * 2
+    scratch += [pltpu.SemaphoreType.DMA((SHIPS,))] * 2
     results = pl.pallas_call(
         functools.partial(reduce_kernel, matrices, units, events, dims),
         out_shape=outs,
-        in_specs=[anywhere] * (4 * len(matrices)) + [vmem],
-        out_specs=[vmem] * len(outs),
+        in_specs=[anywhere] * (2 * count) + [vmem] + [anywhere] * SHIPS,
+        out_specs=[vmem] * len(units) + [anywhere] * (SHIPS + 2 * count) + [vmem],
         scratch_shapes=scratch,
         compiler_params=pltpu.CompilerParams(
             collective_id=0, has_side_effects=True, vmem_limit_bytes=62 * 2**20
@@ -436,7 +912,7 @@
             ]
             whole = jnp.concatenate([whole, jnp.concatenate(parts, axis=1)], axis=0)
         wholes.append(whole)
-    return wholes, results[-1]
+    return wholes, results[-1], results[len(units) : len(units) + SHIPS]
 
 
 def even_cuts(columns, width):
@@ -451,7 +927,7 @@
         Matrix(width // chunks, 3 * width, [1152] * 3, even_cuts(3 * width, 1152)),
         Matrix(2 * width // chunks, width, [640, 512], [(0, 640), (640, 512)]),
     ]
-    units = make_units(matrices, [HOPS[name] for name in HOP_PLAN])
+    units = make_units(matrices, HOP_PLAN)
     return matrices, units, EVENTS
 
 
@@ -471,7 +947,7 @@
     return block
 
 
-def local(
+def local_permutes(
     inputs,
     skipped,
     lengths,
@@ -565,15 +1041,18 @@
     order_y = above + ["seq"]
     order_z = above[1:] + ["seq"] + above[:1]
 
+    grad_fc2 = halving(own_rows(acted_low, grad_out), order_x, bits)
     grad_fc2_bias = column_sum(grad_out)
     grad_acted = matmul(grad_out, fc2_weight.T)
     grad_hidden = gelu_back(grad_acted)[0].astype(jnp.bfloat16)
+    grad_fc1 = halving(own_rows(normed_two, grad_hidden), order_x, bits)
     grad_fc1_bias = column_sum(grad_hidden)
     grad_normed_two = matmul(grad_hidden, fc1_weight.T)
     _, norm_back_two = jax.vjp(layer_norm, stream_two, gain_two, shift_two)
     back_two, grad_gain_two, grad_shift_two = norm_back_two(grad_normed_two)
     grad_stream_two = grad_out.astype(jnp.float32) + back_two
     grad_attended = grad_stream_two.astype(jnp.bfloat16)
+    grad_proj = halving(own_rows(mixed, grad_attended), order_y, bits)
     grad_proj_bias = column_sum(grad_attended)
     grad_mixed = matmul(grad_attended, proj_weight.T)
     grad_mixed = grad_mixed.astype(jnp.bfloat16).reshape(rows, HEADS, HEAD_DIM)
@@ -585,10 +1064,12 @@
     grad_keys = product("hqk,qhd->khd", grad_scores, query) * scale
     grad_packed = jnp.stack([grad_query, grad_keys, grad_values], axis=1)
     grad_packed = grad_packed.astype(jnp.bfloat16).reshape(rows, 3 * width)
+    grad_qkv = halving(own_rows(normed, grad_packed), order_y, bits)
     grad_normed = matmul(grad_packed, qkv_weight.T)
     _, norm_back_one = jax.vjp(layer_norm, stream, gain_one, shift_one)
     back_one, grad_gain_one, grad_shift_one = norm_back_one(grad_normed)
     grad_stream = (grad_stream_two + back_one).astype(jnp.bfloat16)
+    grad_skip = halving(own_rows(joined, grad_stream), order_z, bits)
     grad_skip_bias = column_sum(grad_stream)
     grad_joined = matmul(grad_stream, skip_weight.T)
 
@@ -603,27 +1084,8 @@
         grad_fc2_bias,
     )
     chunks = dp_count * seq_count
-    pairs = [
-        (acted_low, grad_out),
-        (normed_two, grad_hidden),
-        (mixed, grad_attended),
-        (normed, grad_packed),
-        (joined, grad_stream),
-    ]
     line = jnp.concatenate([v.reshape(chunks, -1) for v in vectors], axis=1)
-    used = line.shape[1]
-    if chunks == 32:
-        lines = jnp.pad(line, ((0, 0), (0, 8 * 128 - used)))
-        lines = lines.reshape((2,) * (bits - 1) + (2, 2, 8, 128))
-        lines = jnp.moveaxis(lines, bits - 1, 0)
-        plan = make_plan(width, fc1_weight.shape[1], chunks)
-        weights, line = weight_gradients(pairs, lines, plan, bits)
-        line = line.reshape(-1)
-    else:
-        orders = [order_x, order_x, order_y, order_y, order_z]
-        weights = [halving(own_rows(*p), o, bits) for p, o in zip(pairs, orders)]
-        line = lax.psum_scatter(line, ("dp", "seq"), scatter_dimension=0, tiled=True)[0]
-    grad_fc2, grad_fc1, grad_proj, grad_qkv, grad_skip = weights
+    line = lax.psum_scatter(line, ("dp", "seq"), scatter_dimension=0, tiled=True)[0]
     pieces, start = [], 0
     for vector in vectors:
         size = vector.shape[0] // chunks
@@ -650,9 +1112,97 @@
     )
 
 
+def local_kernels(*arguments):
+    arrays = Arguments(*arguments)
+    items, half, width = arrays.inputs.shape
+    hidden = arrays.fc1_weight.shape[1]
+    dp_count = lax.axis_size("dp")
+    bits = dp_count.bit_length() - 1
+    seq_index = lax.axis_index("seq")
+    device = lax.axis_index("dp") * 2 + seq_index
+    first = seq_index == 0
+    chunks = dp_count * 2
+    skipped = arrays.skipped.reshape(items, 2, half, width // 2)
+    plan = make_plan(width, hidden, chunks)
+    feed = dict(
+        inputs=arrays.inputs,
+        inputs_got=swap_seq(pick(arrays.inputs, 1 - seq_index, 0)),
+        skipped=skipped,
+        skipped_got=swap_seq(pick(skipped, 1 - seq_index, 0)),
+        cotangent=arrays.cotangent,
+        cotangent_got=swap_seq(pick(arrays.cotangent, 1 - seq_index, 0)),
+        lengths=arrays.lengths,
+    )
+    for name in Arguments._fields[4:]:
+        value = getattr(arrays, name)
+        feed[name] = value if value.ndim == 2 else value.reshape(1, -1)
+    found = run_block(feed, plan[0], width, hidden, half)
+    weights, vectors, got = weight_gradients(
+        [getattr(found, name) for name in LEFTS],
+        [getattr(found, name) for name in RIGHTS],
+        found.vectors,
+        [found.block_send, found.grad_in_send, found.grad_skip_send],
+        plan,
+        bits,
+    )
+    block_got, grad_in_got, grad_skip_got = got
+
+    def owner(own, other):
+        other = other.astype(own.dtype)
+        return jnp.where(first, jnp.stack([own, other]), jnp.stack([other, own]))
+
+    share = width // chunks
+    mine = lax.dynamic_slice(vectors, (0, device * share), (8, share))
+    wide_share = hidden // chunks
+    per_row = width // wide_share
+    row = 8 + device // per_row
+    bias = lax.dynamic_slice(vectors, (row, device % per_row * wide_share), (1, wide_share))[0]
+    grad_fc2, grad_fc1, grad_proj, grad_qkv, grad_skip = weights
+    grad_skip_own = found.grad_skip_own.reshape(2 * half, -1)
+    return (
+        owner(found.block_own, block_got),
+        owner(found.grad_in_own, grad_in_got),
+        owner(grad_skip_own, grad_skip_got.reshape(2 * half, -1)),
+        grad_skip,
+        mine[0],
+        mine[1],
+        mine[2],
+        grad_qkv,
+        grad_proj,
+        mine[3],
+        mine[4],
+        mine[5],
+        grad_fc1,
+        bias,
+        grad_fc2,
+        mine[7],
+    )
+
+
+class Arguments(typing.NamedTuple):
+    inputs: jax.Array
+    skipped: jax.Array
+    lengths: jax.Array
+    cotangent: jax.Array
+    skip_weight: jax.Array
+    skip_bias: jax.Array
+    gain_one: jax.Array
+    shift_one: jax.Array
+    qkv_weight: jax.Array
+    proj_weight: jax.Array
+    proj_bias: jax.Array
+    gain_two: jax.Array
+    shift_two: jax.Array
+    fc1_weight: jax.Array
+    fc1_bias: jax.Array
+    fc2_weight: jax.Array
+    fc2_bias: jax.Array
+
+
 def solution(mesh):
+    small = mesh.shape["dp"] == 16
     return jax.shard_map(
-        local,
+        local_kernels if small else local_permutes,
         mesh=mesh,
         in_specs=(
             P("dp", "seq", None),

time: 441 us -> 316 us (0.72); the launches traced: 436 us -> 316 us
  matrix products: 105 us -> 0 us
  Pallas kernels: 187 us -> 268 us
  local copies, waits for them, and re-layouts: 77.5 us -> 14.4 us
  other arithmetic: 36 us -> 9.89 us
  starting transfers between devices: 11.6 us -> 5.15 us
    dot_general x20 -> x0, matrix products: 105 us -> none  [the longest x10 66.3 us: matmul(): return jnp.dot(left, right, preferred_element_type=jnp.float32)]
    pallas_call x0 -> x1, Pallas kernels: none -> 98 us  [run_block(): pl.pallas_call(functools.partial(block_kernel, half, hidden, matrices, na...]
    pallas_call x1, Pallas kernels: 187 us -> 170 us  [weight_gradients(): pl.pallas_call(functools.partial(reduce_kernel, matrices, units, events,...]
    unnamed x164 -> x62, local copies, waits for them, and re-layouts: 15.6 us -> 2.39 us
    squeeze x8 -> x3, local copies, waits for them, and re-layouts: 13.5 us -> 2.17 us  [pick(): return lax.dynamic_index_in_dim(values, index, axis, keepdims=False)]
    convert_element_type x3 -> x0, local copies, waits for them, and re-layouts: 11.1 us -> none  [the longest x1 4.51 us: local(): packed = matmul(normed, qkv_weight).astype(jnp.bfloat16)]
    pad x5 -> x0, local copies, waits for them, and re-layouts: 9.6 us -> none  [weight_gradients(): padded = jnp.pad(right, ((0, LANES - right.shape[0]), (0, 0)))]
    transpose x3 -> x0, local copies, waits for them, and re-layouts: 8.18 us -> none  [the longest x1 4.28 us: left_operand(): return parts.transpose(1, 0, 2, 3, 4).reshape(core_count, -1, LANES)]
  transfers between devices with their start and end apart: 16 -> 3, of which waited for: 3 -> 3; matrix products, arithmetic and copies ran while one was open for 22% -> 2% of each run, Pallas kernels for 0% -> 0%
where the time goes in v3:
time: 316 us
  Pallas kernels  268 us (85%)
  waiting for transfers between devices  17 us (5%)
  local copies, waits for them, and re-layouts  14.4 us (5%)
  other arithmetic  9.89 us (3%)
  starting transfers between devices  5.15 us (2%)
    pallas_call x1, Pallas kernels, weight_gradients(): pl.pallas_call(functools.partial(reduce_kernel, matrices, units, events,...  170 us
    pallas_call x1, Pallas kernels, run_block(): pl.pallas_call(functools.partial(block_kernel, half, hidden, matrices, na...  98 us
    ppermute x3, waiting for transfers between devices, swap_seq(): return lax.ppermute(values, 'seq', [(0, 1), (1, 0)])  17 us
  transfers between devices with their start and end apart: 3, of which 3 were waited for; matrix products, arithmetic and copies ran while one was open for 2% of the time, Pallas kernels for 0%

profile of v3, /device:TPU:0, one launch (start us, length us, event | category | flops | bytes accessed | tf_op | source)
XLA Modules:
  0.0 315.7 jit_solution(9140319615489865244)
XLA Ops:
  0.7 1.1 dynamic-slice_bitcast_fusion
  1.9 3.0 collective-permute-start.1
  4.9 1.0 dynamic-slice_bitcast_fusion.2
  6.0 2.1 collective-permute-start.2
  12.9 2.7 collective-permute-done.1.refs_3_
  15.6 0.8 copy-done.3
  16.4 7.5 %collective-permute-done.refs_1_ = bf16[168,1152]{1,0:T(8,128)(2,1)S(1)} collective-permute-done((bf16[168,1152]{1,0:T(8,128)(2,1)S(1)}, bf16[168,1152]{1,0:T(8,128)(2,1)S(1)}, u32[]{:S(2)}, u32[]{:S(2)}) %collective-permute-start) | collective-permute-done | bytes 387104 | tf_op jit(solution)/shard_map/ppermute | solution.py:41
  24.6 6.7 %collective-permute-done.2.refs_5_ = bf16[168,1152]{1,0:T(8,128)(2,1)S(1)} collective-permute-done((bf16[168,1152]{1,0:T(8,128)(2,1)S(1)}, bf16[168,1152]{1,0:T(8,128)(2,1)S(1)}, u32[]{:S(2)}, u32[]{:S(2)}) %collective-permute-start.2) | collective-permute-done | bytes 387104 | tf_op jit(solution)/shard_map/ppermute | solution.py:41
  31.4 0.8 copy-done.7
  32.1 98.0 %block.1 = (bf16[168,1152]{1,0:T(8,128)(2,1)}, bf16[168,1152]{1,0:T(8,128)(2,1)}, f32[168,1152]{1,0:T(8,128)}, bf16[168,1152]{1,0:T(8,128)(2,1)}, f32[2,168,576]...) custom-call(bf16[2,168,1152]{2,1,0:T(8,128)(2,1)} %refs_0_.1, ...), custom_call_target="tpu_custom_call" | custom-call | tf_op jit(solution)/shard_map/block/pallas_call | solution.py:516
  130.1 170.5 %reduce_weights.1 = (f32[144,384]{1,0:T(8,128)}, f32[144,384]{1,0:T(8,128)}, f32[144,384]{1,0:T(8,128)}, f32[32,1152]{1,0:T(8,128)}, f32[32,1152]{1,0:T(8,128)},...) custom-call(bf16[2,2304,384]{2,1,0:T(8,128)(2,1)} %get-tuple-element, ...), custom_call_target="tpu_custom_call" | custom-call | tf_op jit(solution)/shard_map/reduce_weights/pallas_call | solution.py:892
  300.6 0.8 slice.57
  302.1 0.8 fusion.2
  302.9 1.1 bitcast_convert_fusion
  304.0 1.0 bitcast_convert_fusion.1
  305.0 0.8 constant_dynamic-slice_fusion
  306.4 1.3 maximum_select_fusion
  307.8 1.2 maximum_select_fusion.1
  309.0 1.4 dynamic_slice.21
  310.4 1.1 maximum_select_fusion.2
  311.6 0.9 pad_maximum_fusion
  313.2 0.7 maximum_maximum_fusion.2
  314.0 0.8 maximum_maximum_fusion.1
  314.8 0.9 maximum_maximum_fusion
  (74 shorter events, 7.7 us)
Async XLA Ops:
  0.6 5.3 %copy-start = (bf16[2,168,1152]{2,1,0:T(8,128)(2,1)S(1)}, bf16[2,168,1152]{2,1,0:T(8,128)(2,1)}, u32[]{:S(2)}) copy-start(bf16[2,168,1152]{2,1,0:T(8,128)(2,1)} %refs_4_.1) | copy-start | bytes 2322436
  0.7 7.4 %copy-start.23 = (f32[4608]{0:T(1024)S(1)}, f32[4608]{0:T(1024)}, u32[]{:S(2)}) copy-start(f32[4608]{0:T(1024)} %param.31) | copy-start | bytes 55300
  0.7 8.0 %copy-start.24 = (f32[1152]{0:T(1024)S(1)}, f32[1152]{0:T(1024)}, u32[]{:S(2)}) copy-start(f32[1152]{0:T(1024)} %param.22) | copy-start | bytes 13828
  0.7 8.6 %copy-start.25 = (f32[1152]{0:T(1024)S(1)}, f32[1152]{0:T(1024)}, u32[]{:S(2)}) copy-start(f32[1152]{0:T(1024)} %param.23) | copy-start | bytes 13828
  0.7 9.2 %copy-start.26 = (f32[1152]{0:T(1024)S(1)}, f32[1152]{0:T(1024)}, u32[]{:S(2)}) copy-start(f32[1152]{0:T(1024)} %param.24) | copy-start | bytes 13828
  0.7 9.8 %copy-start.27 = (f32[1152]{0:T(1024)S(1)}, f32[1152]{0:T(1024)}, u32[]{:S(2)}) copy-start(f32[1152]{0:T(1024)} %param.27) | copy-start | bytes 13828
  0.7 10.4 %copy-start.28 = (f32[1152]{0:T(1024)S(1)}, f32[1152]{0:T(1024)}, u32[]{:S(2)}) copy-start(f32[1152]{0:T(1024)} %param.28) | copy-start | bytes 13828
  0.7 11.0 %copy-start.29 = (f32[1152]{0:T(1024)S(1)}, f32[1152]{0:T(1024)}, u32[]{:S(2)}) copy-start(f32[1152]{0:T(1024)} %param.29) | copy-start | bytes 13828
  0.7 11.6 %copy-start.30 = (f32[1152]{0:T(1024)S(1)}, f32[1152]{0:T(1024)}, u32[]{:S(2)}) copy-start(f32[1152]{0:T(1024)} %param.33) | copy-start | bytes 13828
  1.9 13.7 %collective-permute-start.1 = (bf16[2,168,576]{2,1,0:T(8,128)(2,1)S(1)}, bf16[2,168,576]{2,1,0:T(8,128)(2,1)S(1)}, u32[]{:S(2)}, u32[]{:S(2)}) collective-permute-start(bf16[2,168,576]{2,1,0:T(8,128)(2,1)S(1)} %dynamic-slice_bitcast_fusion), channel_id=1, source_target_pairs={{0,1},{1,0},{2,3},{3,2},{4,5},{5,4},{6,7},{7,6},{8,9},{9,8},{10,11... | collective-permute-start | bytes 1161224 | tf_op jit(solution)/shard_map/ppermute | solution.py:41
  5.9 18.0 %collective-permute-start = (bf16[168,1152]{1,0:T(8,128)(2,1)S(1)}, bf16[168,1152]{1,0:T(8,128)(2,1)S(1)}, u32[]{:S(2)}, u32[]{:S(2)}) collective-permute-start(bf16[168,1152]{1,0:T(8,128)(2,1)S(1)} %dynamic-slice_bitcast_fusion.2), channel_id=1, source_target_pairs={{0,1},{1,0},{2,3},{3,2},{4,5},{5,4},{6,7},{7,6},{8,9},{9,8},{10,11... | collective-permute-start | bytes 1161224 | tf_op jit(solution)/shard_map/ppermute | solution.py:41
  6.0 25.3 %collective-permute-start.2 = (bf16[168,1152]{1,0:T(8,128)(2,1)S(1)}, bf16[168,1152]{1,0:T(8,128)(2,1)S(1)}, u32[]{:S(2)}, u32[]{:S(2)}) collective-permute-start(bf16[168,1152]{1,0:T(8,128)(2,1)S(1)} %dynamic-slice_bitcast_fusion.1), channel_id=1, source_target_pairs={{0,1},{1,0},{2,3},{3,2},{4,5},{5,4},{6,7},{7,6},{8,9},{9,8},{10,11... | collective-permute-start | bytes 1161224 | tf_op jit(solution)/shard_map/ppermute | solution.py:41
  300.6 5.8 %copy-start.21 = (f32[16,1152]{1,0:T(8,128)S(1)}, f32[16,1152]{1,0:T(8,128)}, u32[]{:S(2)}) copy-start(f32[16,1152]{1,0:T(8,128)} %get-tuple-element.88) | copy-start | bytes 221188
  300.6 5.8 %copy-start.22 = (f32[16,1152]{1,0:T(8,128)S(1)}, f32[16,1152]{1,0:T(8,128)}, u32[]{:S(2)}) copy-start(f32[16,1152]{1,0:T(8,128)} %get-tuple-element.81) | copy-start | bytes 221188
  300.6 5.8 %copy-start.1 = (f32[2,168,576]{2,1,0:T(8,128)S(1)}, f32[2,168,576]{2,1,0:T(8,128)}, u32[]{:S(2)}) copy-start(f32[2,168,576]{2,1,0:T(8,128)} %get-tuple-element.72) | copy-start | bytes 2322436
  307.7 3.8 %copy-start.8 = (f32[144,384]{1,0:T(8,128)S(1)}, f32[144,384]{1,0:T(8,128)}, u32[]{:S(2)}) copy-start(f32[144,384]{1,0:T(8,128)} %get-tuple-element.89) | copy-start | bytes 663556
  307.8 3.8 %copy-start.9 = (f32[144,384]{1,0:T(8,128)S(1)}, f32[144,384]{1,0:T(8,128)}, u32[]{:S(2)}) copy-start(f32[144,384]{1,0:T(8,128)} %get-tuple-element.90) | copy-start | bytes 663556
  307.8 3.8 %copy-start.10 = (f32[144,384]{1,0:T(8,128)S(1)}, f32[144,384]{1,0:T(8,128)}, u32[]{:S(2)}) copy-start(f32[144,384]{1,0:T(8,128)} %get-tuple-element.91) | copy-start | bytes 663556
  309.0 3.5 %copy-start.19 = (f32[32,1152]{1,0:T(8,128)S(1)}, f32[32,1152]{1,0:T(8,128)}, u32[]{:S(2)}) copy-start(f32[32,1152]{1,0:T(8,128)} %get-tuple-element.82) | copy-start | bytes 442372
  309.0 4.2 %copy-start.11 = (f32[64,640]{1,0:T(8,128)S(1)}, f32[64,640]{1,0:T(8,128)}, u32[]{:S(2)}) copy-start(f32[64,640]{1,0:T(8,128)} %get-tuple-element.74) | copy-start | bytes 491524
  309.0 4.2 %copy-start.20 = (f32[64,512]{1,0:T(8,128)S(1)}, f32[64,512]{1,0:T(8,128)}, u32[]{:S(2)}) copy-start(f32[64,512]{1,0:T(8,128)} %get-tuple-element.75) | copy-start | bytes 393220
  310.4 3.5 %copy-start.16 = (f32[32,1152]{1,0:T(8,128)S(1)}, f32[32,1152]{1,0:T(8,128)}, u32[]{:S(2)}) copy-start(f32[32,1152]{1,0:T(8,128)} %get-tuple-element.78) | copy-start | bytes 442372
  310.4 3.5 %copy-start.17 = (f32[32,1152]{1,0:T(8,128)S(1)}, f32[32,1152]{1,0:T(8,128)}, u32[]{:S(2)}) copy-start(f32[32,1152]{1,0:T(8,128)} %get-tuple-element.79) | copy-start | bytes 442372
  310.4 3.5 %copy-start.18 = (f32[32,1152]{1,0:T(8,128)S(1)}, f32[32,1152]{1,0:T(8,128)}, u32[]{:S(2)}) copy-start(f32[32,1152]{1,0:T(8,128)} %get-tuple-element.80) | copy-start | bytes 442372
  (10 other events, 21.9 us)
